TPU v7x, 512 devices: a whole 4x8x8 slice. The times are simulated.
512 devices in a mesh: band: 32 (over x_lo, y, core), ga: 16 (over x_hi, z).
Axes of the slice: x: 4 (x_hi: 2, x_lo: 2; x = x_hi * 2 + x_lo), y: 8, z: 8, core: 2. Of those that a mesh axis runs over, the one named last changes fastest.
Arguments:
- orbitals: float32 [32, 2, 128, 4096], P('band', None, None, 'ga'), may hold values from -6 to 6
- orbital_tangent: float32 [32, 2, 128, 4096], P('band', None, None, 'ga'), may hold values from -6 to 6
- stick_columns: int32 [4096], replicated, may hold values from 0 to 16383, as said below
- ion_potential: float32 [128, 128, 128], P('ga'), may hold values from -6 to 6
- core_density: float32 [128, 128, 128], P('ga'), may hold values from 0.5 to 2
- positions: float32 [2000, 3], replicated, may hold values from 0 to 40
- z_charge: float32 [2000], replicated, may hold values from 2 to 8
- widths: float32 [2000], replicated, may hold values from 1.5 to 4
- atom_index: int32 [8], replicated, may hold values from 0 to 1999
- direction: int32 [8], replicated, may hold values from 0 to 2
Outputs:
- hessian_product: float32 [32, 2, 128, 4096], P('band', None, None, 'ga')
Inputs may be any that keep to these rules, and one draw needn't show every extreme that they name: `stick_columns`: 4096 distinct columns gx * 128 + gy, among them every column whose signed frequencies satisfy sx^2 + sy^2 <= 32^2, in no particular order.
All inputs are finite; a program needn't handle non-finite values.
Results may differ from a plain program's by a relative error of at most 0.0001.
Values sent between devices are 32-bit elements; how exact they have to be, the bound alone decides.
No kernel may reach another device: no remote copies, remote signals or barrier semaphores. Data moves between devices by JAX's collectives and lax.ppermute only.
A program may use at most 128 MiB of HBM per device.

v0:
```python
import functools
import math

import jax
import jax.numpy as jnp
import ml_dtypes
import numpy as np
from jax import lax
from jax.experimental import pallas as pl
from jax.experimental.pallas import tpu as pltpu
from jax.sharding import Mesh, PartitionSpec as P

N = 128
BANDS = 32
STICKS = 4096
DISP = 8
CUT = N // 4
LINE = 72
SLABS = 68
CELLS = SLABS * LINE
DUMP = 65 * LINE
CELL = 40.0
SLATER = (3.0 / math.pi) ** (1.0 / 3.0)
FACTOR = (2.0 * math.pi / CELL) ** 2
WEIGHT = 4.0 / N**1.5

BAND_AXES = ("xl", "yh", "yl", "core")
GA_AXES = ("xh", "z")
PLANE_AXES = ("xl", "yl", "core", "xh", "z")
SUBS = 8
GROUPS = 16

f32 = jnp.float32
bf16 = jnp.bfloat16


def split_table(table):
    table = np.asarray(table, np.float64)
    high = table.astype(np.float32).astype(ml_dtypes.bfloat16)
    low = (table - high.astype(np.float64)).astype(np.float32).astype(ml_dtypes.bfloat16)
    return np.stack([high, low])


def signed(values):
    return np.where(values >= N // 2, values - N, values)


def angles(rows, columns):
    return 2.0 * np.pi * (np.outer(rows, columns) % N) / N


def plane_of_holder():
    holder = np.arange(N)
    return (holder % GROUPS) * SUBS + holder // GROUPS


def z_inverse_table():
    kept = np.concatenate([np.arange(0, 40), np.arange(96, 128)])
    angle = angles(plane_of_holder(), kept)
    inside = np.abs(signed(kept)) <= CUT
    cosine, sine = np.cos(angle) * inside, np.sin(angle) * inside
    return split_table(np.block([[cosine, -sine], [sine, cosine]]))


def z_forward_table():
    kept = np.concatenate([np.arange(0, 40), np.arange(96, 128)])
    angle = angles(kept, plane_of_holder())
    scale = 1.0 / (WEIGHT * N**3)
    cosine, sine = np.cos(angle) * scale, np.sin(angle) * scale
    return split_table(np.block([[cosine, sine], [-sine, cosine]]))


def box_frequencies(count):
    slot = np.arange(count)
    return slot - CUT, (slot <= 2 * CUT).astype(np.float64)


def y_inverse_table():
    frequency, kept = box_frequencies(LINE)
    angle = angles(frequency, np.arange(N))
    return split_table(np.concatenate([np.cos(angle), np.sin(angle)], 1) * kept[:, None])


def x_inverse_table():
    across = (4 * np.arange(24)[None, :] + np.arange(4)[:, None]).reshape(-1)
    kept = (across <= 2 * CUT).astype(np.float64)
    angle = angles(np.arange(N), across - CUT)
    cosine, sine = WEIGHT * np.cos(angle) * kept, WEIGHT * np.sin(angle) * kept
    return split_table(np.block([[cosine, -sine], [sine, cosine]]))


def x_forward_table():
    frequency, kept = box_frequencies(LINE)
    angle = angles(frequency, np.arange(N))
    cosine, sine = np.cos(angle) * kept[:, None], np.sin(angle) * kept[:, None]
    return split_table(np.block([[cosine, sine], [-sine, cosine]]))


def y_forward_table():
    frequency, kept = box_frequencies(N)
    angle = angles(np.arange(N), frequency)
    return split_table(np.concatenate([np.cos(angle), np.sin(angle)], 1) * np.concatenate([kept, kept])[None, :])


def spread_table():
    table = np.zeros((N, 8, N))
    for band in range(8):
        for part in range(2):
            for eighth in range(8):
                for group in range(4):
                    for half in range(2):
                        table[band * 16 + part * 8 + eighth, eighth, band * 16 + group * 4 + part * 2 + half] = 1.0
    table = table.reshape(N, 8 * N)
    return np.concatenate([table, table]).astype(ml_dtypes.bfloat16)


def real_table():
    row = np.arange(N)
    frequency = np.where(row <= N // 2, row, row - N // 2)
    angle = angles(frequency, np.arange(N))
    values = np.where((row <= N // 2)[:, None], np.cos(angle), np.sin(angle))
    scale = np.where((row == 0) | (row == N // 2), math.sqrt(1.0 / N), math.sqrt(2.0 / N))
    return values * scale[:, None]


def profile_table():
    frequency = np.arange(N) - N // 2
    angle = angles(frequency, np.arange(N))
    return split_table(np.concatenate([np.cos(angle), np.sin(angle)]))


def halves(values):
    high = values.astype(bf16)
    return high, (values - high.astype(f32)).astype(bf16)


def dot(a, b, dims=((1,), (0,))):
    return lax.dot_general(a, b, (dims, ((), ())), preferred_element_type=f32)


def dot3(left, right, dims=((1,), (0,))):
    return dot(left[0], right[0], dims) + (dot(left[0], right[1], dims) + dot(left[1], right[0], dims))


def pair(ref):
    return ref[0], ref[1]


def stick_frequencies(columns):
    across = columns >> 7
    inplane = columns & (N - 1)
    across = jnp.where(across >= N // 2, across - N, across)
    inplane = jnp.where(inplane >= N // 2, inplane - N, inplane)
    return across, inplane


def kept_rows(shape):
    row = lax.broadcasted_iota(jnp.int32, shape, 0)
    return jnp.where(row >= 40, row + 56 - N, row)


def sphere_radius(columns):
    across, inplane = stick_frequencies(columns)
    frequency = kept_rows((LINE, columns.shape[1]))
    return frequency * frequency + (across * across + inplane * inplane)


def lines_kernel(orbital_ref, tangent_ref, columns_ref, table_ref, out_ref):
    inside = sphere_radius(columns_ref[...]) <= CUT * CUT
    for which, ref in enumerate((orbital_ref, tangent_ref)):
        parts = []
        for part in range(2):
            kept = jnp.concatenate([ref[0, part, 0:40, :], ref[0, part, 96:128, :]], 0)
            parts.append(jnp.where(inside, kept, 0.0))
        lines = dot3(pair(table_ref), halves(jnp.concatenate(parts, 0)))
        for part in range(2):
            for half in range(2):
                row = half * 4 + which * 2 + part
                out_ref[pl.ds(row, N, stride=8), :] = lines[part * N : (part + 1) * N, half * N : (half + 1) * N]


def fields_kernel(
    dest_ref, lines_ref, ytable_ref, xtable_ref, real_ref, realt_ref, fields_ref, sums_ref, spectrum_ref, turned, grid, ycos, ysin
):
    for block in range(8):
        tiles = [lines_ref[sub * GROUPS + 2 * block + odd] for odd in range(2) for sub in range(SUBS)]
        turned[block * N : (block + 1) * N, :] = jnp.concatenate(tiles, 0).T
    grid[...] = jnp.zeros_like(grid)
    lane = lax.broadcasted_iota(jnp.int32, (1, N), 1)
    group = (lane // 64) * 2 + (lane // 4) % 2
    masks = [group == slot for slot in range(4)]
    for block in range(8):

        def scatter(step, carry, block=block):
            for inner in range(8):
                stick = step * 8 + inner
                row = turned[pl.ds(block * N + stick, 1), :]
                for slot in range(4):
                    place = dest_ref[(2 * block + slot // 2) * 256 + (slot % 2) * N + stick]
                    grid[pl.ds(place, 1), :] = jnp.where(masks[slot], row, 0.0)
            return carry

        lax.fori_loop(0, N // 8, scatter, 0)
    lane = lax.broadcasted_iota(jnp.int32, (LINE, N), 1)
    group = (lane // 64) * 2 + (lane // 4) % 2
    first_half = (lane // 4) % 2 == 0
    blank = jnp.zeros((N, N), f32)
    for step in range(17, 24):
        ycos[step * N : (step + 1) * N, :] = blank
        ysin[step * N : (step + 1) * N, :] = blank

    ytable = pair(ytable_ref)
    for step in range(17):
        packed = None
        for slot in range(4):
            slab = grid[(4 * step + slot) * LINE : (4 * step + slot + 1) * LINE, :]
            slab = slab + pltpu.roll(slab, 64, 1)
            slab = slab + jnp.where(first_half, pltpu.roll(slab, N - 4, 1), pltpu.roll(slab, 4, 1))
            packed = slab if packed is None else jnp.where(group == slot, slab, packed)
        lines = dot3(halves(packed.T), ytable)
        ycos[step * N : (step + 1) * N, :] = lines[:, 0:N]
        ysin[step * N : (step + 1) * N, :] = lines[:, N : 2 * N]
    density = jnp.zeros((N, N), f32)
    response = jnp.zeros((N, N), f32)
    xtable = pair(xtable_ref)
    for band in range(SUBS):
        sides = []
        for which in range(2):
            real, imag = [], []
            for slot in range(4):
                base = (slot // 2) * 64 + band * 8 + (slot % 2) * 4 + which * 2
                rows = [pl.ds(base + part, 24, stride=N) for part in range(2)]
                real.append(ycos[rows[0], :] - ysin[rows[1], :])
                imag.append(ysin[rows[0], :] + ycos[rows[1], :])
            sides.append(jnp.concatenate(real + imag, 0))
        field = dot3(xtable, halves(jnp.concatenate(sides, 1)))
        fields_ref[band] = field
        first, second = field[:, 0:N], field[:, N : 2 * N]
        density = density + first[0:N] * first[0:N] + first[N : 2 * N] * first[N : 2 * N]
        response = response + first[0:N] * second[0:N] + first[N : 2 * N] * second[N : 2 * N]
    response = response * (2.0 / BANDS)
    sums_ref[0] = density * (1.0 / BANDS)
    sums_ref[1] = response
    spectrum_ref[...] = dot3(halves(dot3(pair(real_ref), halves(response))), pair(realt_ref))


def hartree_kernel(place_ref, columns_ref, real_ref, back_ref, out_ref):
    four = [columns_ref[pl.ds(slot, N, stride=4), :] for slot in range(4)]
    lines = dot3(pair(real_ref), halves(jnp.concatenate(four, 1)))
    shape = (N, 4 * N)
    row = lax.broadcasted_iota(jnp.int32, shape, 0)
    lane = lax.broadcasted_iota(jnp.int32, shape, 1)
    across = place_ref[0] * 4 + lane // N
    inplane = lane % N

    def frequency(index):
        return jnp.where(index <= N // 2, index, index - N // 2)

    across, inplane, row = frequency(across), frequency(inplane), frequency(row)
    squares = (row * row + across * across + inplane * inplane).astype(f32)
    kernel = jnp.where(squares == 0.0, 0.0, (4.0 * math.pi / FACTOR) / jnp.where(squares == 0.0, 1.0, squares))
    back = dot3(halves(back_ref[...]), halves(lines * kernel))
    for slot in range(4):
        part = back[:, slot * N : (slot + 1) * N]
        for copy in range(4):
            for x_low in range(2):
                base = ((x_low * 4 + copy) * 4) * 4 + slot
                out_ref[pl.ds(base, 4, stride=4), :] = part[x_low * 4 : (x_low + 1) * 4]


def ions_kernel(place_ref, atom_ref, direction_ref, positions_ref, charge_ref, widths_ref, table_ref, out_ref, centres, spreads, marks, charges):
    for slot in range(DISP):
        atom = atom_ref[slot]
        charges[slot : slot + 1, :] = jnp.full((1, N), charge_ref[atom] * (-1.0 / CELL), f32)
        for axis in range(3):
            row = axis * DISP + slot
            centres[row : row + 1, :] = jnp.full((1, N), positions_ref[atom * 3 + axis], f32)
            spreads[row : row + 1, :] = jnp.full((1, N), widths_ref[atom], f32)
            marks[row : row + 1, :] = jnp.full((1, N), jnp.where(direction_ref[slot] == axis, 1.0, 0.0), f32)
    frequency = lax.broadcasted_iota(jnp.int32, (3 * DISP, N), 1) - N // 2
    wavenum = frequency.astype(f32) * (2.0 * math.pi / CELL)
    damping = jnp.exp(-0.5 * (wavenum * spreads[...]) ** 2)
    phase = wavenum * centres[...]
    cosine, sine = damping * jnp.cos(phase), damping * jnp.sin(phase)
    chosen = marks[...] > 0.5
    with_cos = jnp.where(chosen, -wavenum * sine, cosine)
    with_sin = jnp.where(chosen, wavenum * cosine, sine)
    profiles = dot3(halves(jnp.concatenate([with_cos, with_sin], 1)), pair(table_ref))
    along_x, along_y, along_z = profiles[0:8], profiles[8:16], profiles[16:24]
    lane = lax.broadcasted_iota(jnp.int32, (DISP, N), 1)
    here = jnp.sum(jnp.where(lane == place_ref[1], along_z, 0.0), 1, keepdims=True)
    scaled = along_y * here * charges[...]
    padding = jnp.zeros((N - DISP, N), f32)
    left = jnp.concatenate([along_x, padding], 0).T
    right = jnp.concatenate([scaled, padding], 0)
    out_ref[...] = dot3(halves(left), halves(right))


def products_kernel(
    place_ref,
    dest_ref,
    fields_ref,
    sums_ref,
    hartree_ref,
    ions_ref,
    potential_ref,
    core_ref,
    real_ref,
    realt_ref,
    xtable_ref,
    ytable_ref,
    spread_ref,
    out_ref,
    lines,
    grid,
    gathered,
):
    density = (sums_ref[0, 0] + sums_ref[1, 0]) + (sums_ref[2, 0] + sums_ref[3, 0])
    response = (sums_ref[0, 1] + sums_ref[1, 1]) + (sums_ref[2, 1] + sums_ref[3, 1])
    hartree = dot3(halves(dot3(pair(realt_ref), halves(hartree_ref[...]))), pair(real_ref))
    total = density + core_ref[0]
    root = jnp.exp(jnp.log(total) * (1.0 / 3.0))
    exchange = -SLATER * root
    effective = potential_ref[0] + exchange
    change = exchange / (3.0 * total) * response + hartree + ions_ref[...]
    xtable = pair(xtable_ref)
    ytable = pair(ytable_ref)
    effective2 = jnp.concatenate([effective, effective], 0)
    change2 = jnp.concatenate([change, change], 0)
    blocks = [[], []]
    for couple in range(SUBS // 2):
        sides = []
        for band in (2 * couple, 2 * couple + 1):
            sides.append(effective2 * fields_ref[band, :, N : 2 * N] + change2 * fields_ref[band, :, 0:N])
        across = dot3(xtable, halves(jnp.concatenate(sides, 1)))
        rows = jnp.concatenate([across[:, 0:N], across[:, N : 2 * N]], 0)
        done = dot3(halves(rows), ytable)
        for side in range(2):
            real = done[side * 144 : side * 144 + 72]
            imag = done[side * 144 + 72 : side * 144 + 144]
            base = (2 * couple + side) * 144
            lines[base : base + 72, :] = real[:, 0:N] + imag[:, N : 2 * N]
            lines[base + 72 : base + 144, :] = imag[:, 0:N] - real[:, N : 2 * N]
    spread = spread_ref[...]
    for eight in range(9):
        tiles = [lines[half * 72 + eight * 8 : half * 72 + eight * 8 + 8, :] for half in range(16)]
        turned = jnp.concatenate(tiles, 0).T[0:LINE]
        high, low = halves(turned)
        cells = dot(jnp.concatenate([high, low], 1), spread)
        for eighth in range(8):
            base = (eight * 8 + eighth) * LINE
            grid[base : base + LINE, :] = cells[:, eighth * N : (eighth + 1) * N]
    lane = lax.broadcasted_iota(jnp.int32, (1, N), 1)
    slot_of_lane = ((lane // 4) % 4) * 2 + lane % 2
    masks = [slot_of_lane == slot for slot in range(1, 8)]
    for block in range(4):

        def gather(step, carry, block=block):
            for inner in range(8):
                stick = step * 8 + inner
                row = None
                for slot in range(8):
                    place = dest_ref[(4 * block + slot // 2) * 256 + (slot % 2) * N + stick]
                    cell = grid[pl.ds(place, 1), :]
                    row = cell if slot == 0 else jnp.where(masks[slot - 1], cell, row)
                gathered[pl.ds(stick, 1), :] = row
            return carry

        lax.fori_loop(0, N // 8, gather, 0)
        turned = gathered[...].T
        for band in range(SUBS):
            base = band * 64 + block * 16
            out_ref[base : base + 16, :] = turned[band * 16 : band * 16 + 16]


def result_kernel(arrived_ref, tangent_ref, columns_ref, table_ref, out_ref):
    sides = []
    for half in range(2):
        parts = [arrived_ref[pl.ds(part * 2 + half, N, stride=4), :] for part in range(2)]
        sides.append(jnp.concatenate(parts, 0))
    lines = dot3(pair(table_ref), halves(jnp.concatenate(sides, 1)))
    radius = sphere_radius(columns_ref[...])
    inside = radius <= CUT * CUT
    kinetic = (0.5 * FACTOR) * radius.astype(f32)
    for part in range(2):
        kept = jnp.concatenate([tangent_ref[0, part, 0:40, :], tangent_ref[0, part, 96:128, :]], 0)
        rows = jnp.where(inside, lines[part * LINE : (part + 1) * LINE] + kinetic * kept, 0.0)
        out_ref[0, part, 0:40, :] = rows[0:40]
        out_ref[0, part, 40:96, :] = jnp.zeros((56, 256), f32)
        out_ref[0, part, 96:128, :] = rows[40:72]


def vmem(count):
    return [pl.BlockSpec(memory_space=pltpu.VMEM)] * count


def smem(count):
    return [pl.BlockSpec(memory_space=pltpu.SMEM)] * count


def shape(*dims):
    return jax.ShapeDtypeStruct(dims, f32)


def params(mebibytes):
    return pltpu.CompilerParams(vmem_limit_bytes=mebibytes << 20)


def body(
    orbitals,
    orbital_tangent,
    stick_columns,
    ion_potential,
    core_density,
    positions,
    z_charge,
    widths,
    atom_index,
    direction,
):
    group = lax.axis_index(GA_AXES)
    member = lax.axis_index(BAND_AXES)
    sub = lax.axis_index(("xl", "yl", "core"))
    plane = group * SUBS + sub
    place = jnp.stack([member, plane]).astype(jnp.int32)
    columns = lax.dynamic_slice_in_dim(stick_columns, group * 256, 256).reshape(1, 256)
    across, inplane = stick_frequencies(stick_columns)
    cell = (across + CUT) * LINE + (inplane + CUT)
    dest = jnp.where(across * across + inplane * inplane <= CUT * CUT, cell, DUMP)
    real = split_table(real_table())
    realt = split_table(real_table().T)

    lines = pl.pallas_call(
        lines_kernel, out_shape=shape(N * 8, N), in_specs=vmem(4), out_specs=vmem(1)[0], name="lines"
    )(orbitals, orbital_tangent, columns, z_inverse_table())
    lines = lax.all_to_all(lines.reshape(N, 8, N), PLANE_AXES, 0, 0, tiled=True)
    ions = pl.pallas_call(
        ions_kernel,
        out_shape=shape(N, N),
        in_specs=smem(6) + vmem(1),
        out_specs=vmem(1)[0],
        scratch_shapes=[pltpu.VMEM((24, N), f32)] * 3 + [pltpu.VMEM((8, N), f32)],
        name="ions",
    )(place, atom_index, direction, positions.reshape(-1), z_charge, widths, profile_table())
    fields, sums, spectrum = pl.pallas_call(
        fields_kernel,
        out_shape=(shape(SUBS, 2 * N, 2 * N), shape(2, N, N), shape(N, N)),
        in_specs=smem(1) + vmem(5),
        out_specs=tuple(vmem(3)),
        scratch_shapes=[
            pltpu.VMEM((8 * N, N), f32),
            pltpu.VMEM((CELLS, N), f32),
            pltpu.VMEM((24 * N, N), f32),
            pltpu.VMEM((24 * N, N), f32),
        ],
        compiler_params=params(32),
        name="fields",
    )(dest, lines, y_inverse_table(), x_inverse_table(), real, realt)
    sums = lax.all_gather(sums, "yh")
    arrived = lax.all_to_all(spectrum.reshape(32, 4, N), BAND_AXES, 0, 0, tiled=True)
    arrived = arrived.reshape(2, 4, 4, 4, N).sum(1).reshape(1, 8 * 4, N)
    arrived = jnp.broadcast_to(arrived, (GROUPS, 32, N))
    columns_here = lax.all_to_all(arrived, GA_AXES, 0, 0, tiled=True).reshape(4 * N, N)
    back = lax.dynamic_slice_in_dim(jnp.asarray(real_table().T, f32), group * SUBS, SUBS)
    solved = pl.pallas_call(
        hartree_kernel,
        out_shape=shape(N, N),
        in_specs=smem(1) + vmem(3),
        out_specs=vmem(1)[0],
        name="hartree",
    )(place, columns_here, real, back)
    solved = lax.all_to_all(solved.reshape(32, 4, N), BAND_AXES, 0, 0, tiled=True).reshape(N, N)
    potential = lax.dynamic_slice_in_dim(ion_potential, sub, 1)
    core = lax.dynamic_slice_in_dim(core_density, sub, 1)
    outgoing = pl.pallas_call(
        products_kernel,
        out_shape=shape(4 * N, N),
        in_specs=smem(2) + vmem(11),
        out_specs=vmem(1)[0],
        scratch_shapes=[
            pltpu.VMEM((16 * LINE, N), f32),
            pltpu.VMEM((LINE * LINE, N), f32),
            pltpu.VMEM((N, N), f32),
        ],
        compiler_params=params(32),
        name="products",
    )(
        place,
        dest,
        fields,
        sums,
        solved,
        ions,
        potential,
        core,
        real,
        realt,
        x_forward_table(),
        y_forward_table(),
        spread_table(),
    )
    arrived = lax.all_to_all(outgoing.reshape(N, 4, N), PLANE_AXES, 0, 0, tiled=True).reshape(4 * N, N)
    return pl.pallas_call(
        result_kernel, out_shape=shape(1, 2, N, 256), in_specs=vmem(4), out_specs=vmem(1)[0], name="result"
    )(arrived, orbital_tangent, columns, z_forward_table())


def solution(mesh):
    fine = Mesh(mesh.devices.reshape(2, 4, 2, 2, 2, 8), BAND_AXES + GA_AXES)
    lines = P(BAND_AXES, None, None, GA_AXES)
    planes = P(GA_AXES, None, None)
    return jax.shard_map(
        body,
        mesh=fine,
        in_specs=(lines, lines, P(), planes, planes, P(), P(), P(), P(), P()),
        out_specs=lines,
        check_vma=False,
    )
```

profile of v0, /device:TPU:1, one launch (start us, length us, event | category | flops | bytes accessed | tf_op | source)
XLA Modules:
  0.0 145.1 jit_solution(17001514413113103063)
XLA Ops:
  0.0 0.0 copy-start
  0.0 0.0 copy-start.4
  0.0 0.0 copy-start.5
  0.0 0.0 copy-start.9
  0.0 0.0 copy-start.13
  0.0 1.4 dynamic_slice.12
  1.4 0.0 copy-start.12
  1.4 2.3 %lines.1 = f32[1024,128]{1,0:T(8,128)} custom-call(f32[1,2,128,256]{3,2,1,0:T(8,128)} %orbital_ref.1, f32[1,2,128,256]{3,2,1,0:T(8,128)} %tangent_ref.3, s32[1,256]{1,0:T(1,128)} %bitcast.23, bf16[2,256,144]{2,1,0:T(8,128)(2,1)} %constant.84.clone.table_ref), custom_call_target="tpu_custom_call" | custom-call | tf_op jit(solution)/shard_map/lines/pallas_call | solution.py:433
  3.7 16.6 %all-to-all-start = ((f32[128,8,128]{2,1,0:T(8,128)}), f32[128,8,128]{2,1,0:T(8,128)S(1)}, u32[]{:S(2)}, u32[]{:S(2)}) async-start(f32[128,8,128]{2,1,0:T(8,128)} %bitcast.17), calls=%async_computation | async-start | bytes 1048576 | tf_op jit(solution)/shard_map/all_to_all | solution.py:436
  20.4 0.0 copy-done.13
  20.4 19.2 %all-to-all-done.lines_ref = f32[128,8,128]{2,1,0:T(8,128)S(1)} async-done(((f32[128,8,128]{2,1,0:T(8,128)}), f32[128,8,128]{2,1,0:T(8,128)S(1)}, u32[]{:S(2)}, u32[]{:S(2)}) %all-to-all-start) | async-done | bytes 524320 | tf_op jit(solution)/shard_map/all_to_all | solution.py:436
  39.6 0.0 copy-done
  39.6 0.0 copy-done.4
  39.6 0.0 copy-done.5
  39.6 0.0 copy-done.9
  39.6 10.7 %fields.1 = (f32[8,256,256]{2,1,0:T(8,128)S(1)}, f32[2,128,128]{2,1,0:T(8,128)S(1)}, f32[128,128]{1,0:T(8,128)S(1)}) custom-call(s32[4096]{0:T(1024)S(1)} %add_select_fusion.dest_ref, f32[128,8,128]{2,1,0:T(8,128)S(1)} %all-to-all-done.lines_ref, bf16[2,72,256]{2,1,0:T(8,128)(2,1)S(1)} %copy-done.9, bf16[2,256,192]{2,1,0:T(8,128)(2,1)S(1)} %copy-done.5, ...), custom_call_target="tpu_custom_call" | custom-call | tf_op jit(solution)/shard_map/fields/pallas_call | solution.py:445
  50.3 0.0 copy-start.8
  50.3 14.8 %all_to_all.25 = f32[32,4,128]{2,1,0:T(4,128)S(1)} all-to-all(f32[32,4,128]{2,1,0:T(4,128)S(1)} %bitcast.16), channel_id=1, replica_groups=mesh['xl'=2,'yh'=4,'yl'=2,'core'=2,'xh'=2,'z'=8] {'xl','yh','yl','core'}, dimensions={0} | all-to-all | bytes 131072 | tf_op jit(solution)/shard_map/all_to_all | solution.py:460
  65.1 0.0 copy-done.8
  65.2 0.7 broadcast_in_dim.13
  65.9 0.0 copy-start.1
  65.9 0.0 copy-start.2
  65.9 3.9 %all-to-all-start.2 = ((f32[16,32,128]{2,1,0:T(8,128)}), f32[16,32,128]{2,1,0:T(8,128)S(1)}, u32[]{:S(2)}, u32[]{:S(2)}) async-start(f32[16,32,128]{2,1,0:T(8,128)} %broadcast_in_dim.13), calls=%async_computation.2 | async-start | bytes 524288 | tf_op jit(solution)/shard_map/all_to_all | solution.py:463
  69.8 0.0 copy-done.12
  69.8 1.3 copy.23
  71.1 2.5 %reshape.39.positions_ref = f32[6000]{0:T(1024)} reshape(f32[2000,3]{1,0:T(8,128)} %copy.23) | data formatting | bytes 48000 | tf_op jit(solution)/shard_map/reshape | solution.py:444
  73.6 0.7 pad_add_fusion.place_ref
  74.3 2.5 %ions.1.ions_ref = f32[128,128]{1,0:T(8,128)} custom-call(s32[2]{0:T(128)} %pad_add_fusion.place_ref, s32[8]{0:T(128)} %atom_ref.1, s32[8]{0:T(128)} %direction_ref.1, f32[6000]{0:T(1024)} %reshape.39.positions_ref, f32[2000]{0:T(1024)} %charge_ref.1, f32[2000]{0:T(1024)} %widths_ref.1, bf16[2,256,128]{2,1,0:T(8,128)(2,1)} %constant.85.clone.table_ref), custom_call_target="tpu_custom_call" | custom-call | tf_op jit(solution)/shard_map/ions/pallas_call | solution.py:437
  76.8 1.3 constant_dynamic-slice_fusion.2.back_ref
  78.0 0.9 constant_dynamic-slice_fusion
  78.9 0.2 all-to-all-done.2
  79.1 0.0 copy-start.11
  79.1 0.7 copy-done.11
  79.8 2.0 %hartree.1 = f32[128,128]{1,0:T(8,128)} custom-call(s32[2]{0:T(128)} %pad_add_fusion.place_ref, f32[512,128]{1,0:T(8,128)} %bitcast.19, bf16[2,128,128]{2,1,0:T(8,128)(2,1)} %constant.88.clone.real_ref, f32[8,128]{1,0:T(8,128)} %constant_dynamic-slice_fusion.2.back_ref), custom_call_target="tpu_custom_call" | custom-call | tf_op jit(solution)/shard_map/hartree/pallas_call | solution.py:465
  81.8 6.7 %all-to-all-start.3 = ((f32[32,4,128]{2,1,0:T(4,128)}), f32[32,4,128]{2,1,0:T(4,128)S(1)}, u32[]{:S(2)}, u32[]{:S(2)}) async-start(f32[32,4,128]{2,1,0:T(4,128)} %bitcast.20), calls=%async_computation.3 | async-start | bytes 131072 | tf_op jit(solution)/shard_map/all_to_all | solution.py:472
  88.5 16.9 %all-gather = f32[8,128,128]{2,1,0:T(8,128)S(1)} all-gather(f32[2,128,128]{2,1,0:T(8,128)} %copy-done.8), channel_id=2, replica_groups=mesh['xl'=2,'yh'=4,'yl'=2,'core'=2,'xh'=2,'z'=8] {'yh'}, dimensions={0}, use_global_device_ids=true | all-gather | bytes 655360 | tf_op jit(solution)/shard_map/all_gather | solution.py:459
  105.4 0.0 all-to-all-done.3
  105.4 0.0 copy-done.1
  105.4 0.0 copy-done.2
  105.4 0.0 copy-start.3
  105.4 0.8 copy-done.3
  106.2 0.0 copy-start.6
  106.2 0.9 copy-done.6
  107.1 0.9 copy-done.7
  108.0 0.7 copy-done.10
  108.7 7.3 %products.1 = f32[512,128]{1,0:T(8,128)S(1)} custom-call(s32[2]{0:T(128)S(1)} %copy-done.10, s32[4096]{0:T(1024)S(1)} %add_select_fusion.dest_ref, f32[8,256,256]{2,1,0:T(8,128)S(1)} %get-tuple-element.8.fields_ref, f32[4,2,128,128]{3,2,1,0:T(8,128)S(1)} %bitcast.13, f32[128,128]{1,0:T(8,128)S(1)} %bitcast.15, f32[128,128]{1,0:T(8,128)S(1)} %copy-done.3, ...), custom_call_target="tpu_custom_call" | custom-call | tf_op jit(solution)/shard_map/products/pallas_call | solution.py:475
  116.0 27.1 %all_to_all.26 = f32[128,4,128]{2,1,0:T(4,128)} all-to-all(f32[128,4,128]{2,1,0:T(4,128)S(1)} %bitcast.14), channel_id=1, replica_groups=mesh['xl'=2,'yh'=4,'yl'=2,'core'=2,'xh'=2,'z'=8] {'xl','yl','core','xh',..., dimensions={0} | all-to-all | bytes 524288 | tf_op jit(solution)/shard_map/all_to_all | solution.py:502
  143.1 2.0 %result.1 = f32[1,2,128,256]{3,2,1,0:T(8,128)} custom-call(f32[512,128]{1,0:T(8,128)} %bitcast.18, f32[1,2,128,256]{3,2,1,0:T(8,128)} %tangent_ref.3, s32[1,256]{1,0:T(1,128)} %bitcast.24, bf16[2,144,256]{2,1,0:T(8,128)(2,1)} %constant.94.clone.table_ref), custom_call_target="tpu_custom_call" | custom-call | tf_op jit(solution)/shard_map/result/pallas_call | solution.py:503
  (4 shorter events, 0.0 us)
Async XLA Ops:
  0.0 39.6 %copy-start = (bf16[2,128,128]{2,1,0:T(8,128)(2,1)S(1)}, bf16[2,128,128]{2,1,0:T(8,128)(2,1)}, u32[]{:S(2)}) copy-start(bf16[2,128,128]{2,1,0:T(8,128)(2,1)} %constant.88.clone.real_ref) | copy-start | bytes 196612
  0.0 39.6 %copy-start.4 = (bf16[2,128,128]{2,1,0:T(8,128)(2,1)S(1)}, bf16[2,128,128]{2,1,0:T(8,128)(2,1)}, u32[]{:S(2)}) copy-start(bf16[2,128,128]{2,1,0:T(8,128)(2,1)} %constant.89.clone.realt_ref) | copy-start | bytes 196612
  0.0 39.6 %copy-start.5 = (bf16[2,256,192]{2,1,0:T(8,128)(2,1)S(1)}, bf16[2,256,192]{2,1,0:T(8,128)(2,1)}, u32[]{:S(2)}) copy-start(bf16[2,256,192]{2,1,0:T(8,128)(2,1)} %constant.87.clone.xtable_ref) | copy-start | bytes 589828
  0.0 39.6 %copy-start.9 = (bf16[2,72,256]{2,1,0:T(8,128)(2,1)S(1)}, bf16[2,72,256]{2,1,0:T(8,128)(2,1)}, u32[]{:S(2)}) copy-start(bf16[2,72,256]{2,1,0:T(8,128)(2,1)} %constant.86.clone.ytable_ref) | copy-start | bytes 221188
  0.0 20.4 %copy-start.13 = (s32[4096]{0:T(1024)S(1)}, s32[4096]{0:T(1024)}, u32[]{:S(2)}) copy-start(s32[4096]{0:T(1024)} %param.23) | copy-start | bytes 49156
  1.4 68.4 %copy-start.12 = (f32[2000,3]{0,1:T(4,128)S(1)}, f32[2000,3]{0,1:T(4,128)}, u32[]{:S(2)}) copy-start(f32[2000,3]{0,1:T(4,128)} %param.26) | copy-start | bytes 72004
  3.7 35.9 %all-to-all-start = ((f32[128,8,128]{2,1,0:T(8,128)}), f32[128,8,128]{2,1,0:T(8,128)S(1)}, u32[]{:S(2)}, u32[]{:S(2)}) async-start(f32[128,8,128]{2,1,0:T(8,128)} %bitcast.17), calls=%async_computation | async-start | bytes 1048576 | tf_op jit(solution)/shard_map/all_to_all | solution.py:436
  50.3 14.8 %copy-start.8 = (f32[2,128,128]{2,1,0:T(8,128)}, f32[2,128,128]{2,1,0:T(8,128)S(1)}, u32[]{:S(2)}) copy-start(f32[2,128,128]{2,1,0:T(8,128)S(1)} %get-tuple-element.9) | copy-start | bytes 393220
  65.9 39.5 %copy-start.1 = (bf16[2,128,128]{2,1,0:T(8,128)(2,1)S(1)}, bf16[2,128,128]{2,1,0:T(8,128)(2,1)}, u32[]{:S(2)}) copy-start(bf16[2,128,128]{2,1,0:T(8,128)(2,1)} %constant.88.clone.real_ref) | copy-start | bytes 196612
  65.9 39.5 %copy-start.2 = (bf16[256,1024]{1,0:T(8,128)(2,1)S(1)}, bf16[256,1024]{1,0:T(8,128)(2,1)}, u32[]{:S(2)}) copy-start(bf16[256,1024]{1,0:T(8,128)(2,1)} %constant.93.clone.spread_ref) | copy-start | bytes 1572868
  65.9 13.2 %all-to-all-start.2 = ((f32[16,32,128]{2,1,0:T(8,128)}), f32[16,32,128]{2,1,0:T(8,128)S(1)}, u32[]{:S(2)}, u32[]{:S(2)}) async-start(f32[16,32,128]{2,1,0:T(8,128)} %broadcast_in_dim.13), calls=%async_computation.2 | async-start | bytes 524288 | tf_op jit(solution)/shard_map/all_to_all | solution.py:463
  79.1 0.7 copy-start.11
  81.8 23.5 %all-to-all-start.3 = ((f32[32,4,128]{2,1,0:T(4,128)}), f32[32,4,128]{2,1,0:T(4,128)S(1)}, u32[]{:S(2)}, u32[]{:S(2)}) async-start(f32[32,4,128]{2,1,0:T(4,128)} %bitcast.20), calls=%async_computation.3 | async-start | bytes 131072 | tf_op jit(solution)/shard_map/all_to_all | solution.py:472
  105.4 0.8 copy-start.3
  106.2 0.9 copy-start.6
  107.1 0.9 copy-start.7
  108.0 0.7 copy-start.10
where the time goes:
time: 146 us; the launch traced here: 145 us
  blocking collectives  58.7 us (40%)
  starting transfers between devices  27.2 us (19%)
  Pallas kernels  26.8 us (18%)
  waiting for transfers between devices  19.4 us (13%)
  local copies, waits for them, and re-layouts  12.1 us (8%)
    all_to_all x1, blocking collectives, body(): lax.all_to_all(outgoing.reshape(N, 4, N), PLANE_AXES, 0, 0, tiled=True)  27.1 us
    all_to_all x1, waiting for transfers between devices, body(): lines = lax.all_to_all(lines.reshape(N, 8, N), PLANE_AXES, 0, 0, tiled=True)  19.2 us
    all_gather x1, blocking collectives, body(): sums = lax.all_gather(sums, 'yh')  16.9 us
    all_to_all x1, starting transfers between devices, body(): lines = lax.all_to_all(lines.reshape(N, 8, N), PLANE_AXES, 0, 0, tiled=True)  16.6 us
    all_to_all x1, blocking collectives, body(): lax.all_to_all(spectrum.reshape(32, 4, N), BAND_AXES, 0, 0, tiled=True)  14.8 us
    pallas_call x1, Pallas kernels, body(): pl.pallas_call(fields_kernel, out_shape=(shape(SUBS, 2 * N, 2 * N), shape...  10.7 us
    pallas_call x1, Pallas kernels, body(): pl.pallas_call(products_kernel, out_shape=shape(4 * N, N), in_specs=smem(...  7.26 us
    all_to_all x1, starting transfers between devices, body(): lax.all_to_all(solved.reshape(32, 4, N), BAND_AXES, 0, 0, tiled=True)  6.66 us
  transfers between devices with their start and end apart: 3, of which 2 were waited for; matrix products, arithmetic and copies ran while one was open for 5% of the time, Pallas kernels for 2%

commit v1 on v0

v1 whole, which is shorter than its diff:
```python
import functools
import math

import jax
import jax.numpy as jnp
import ml_dtypes
import numpy as np
from jax import lax
from jax.experimental import pallas as pl
from jax.experimental.pallas import tpu as pltpu
from jax.sharding import Mesh, PartitionSpec as P

N = 128
BANDS = 32
STICKS = 4096
DISP = 8
CUT = N // 4
LINE = 72
SLABS = 68
CELLS = SLABS * LINE
DUMP = 65 * LINE
CELL = 40.0
SLATER = (3.0 / math.pi) ** (1.0 / 3.0)
FACTOR = (2.0 * math.pi / CELL) ** 2
WEIGHT = 4.0 / N**1.5

BAND_AXES = ("xl", "yh", "yl", "core")
GA_AXES = ("xh", "z")
PLANE_AXES = ("xl", "yl", "core", "xh", "z")
SUBS = 8
PITCH = 136
GROUPS = 16

f32 = jnp.float32
bf16 = jnp.bfloat16


def split_table(table):
    table = np.asarray(table, np.float64)
    high = table.astype(np.float32).astype(ml_dtypes.bfloat16)
    low = (table - high.astype(np.float64)).astype(np.float32).astype(ml_dtypes.bfloat16)
    return np.stack([high, low])


def signed(values):
    return np.where(values >= N // 2, values - N, values)


def angles(rows, columns):
    return 2.0 * np.pi * (np.outer(rows, columns) % N) / N


def plane_of_holder():
    holder = np.arange(N)
    return (holder % GROUPS) * SUBS + holder // GROUPS


def z_inverse_table():
    kept = np.concatenate([np.arange(0, 40), np.arange(96, 128)])
    angle = angles(plane_of_holder(), kept)
    inside = np.abs(signed(kept)) <= CUT
    cosine, sine = np.cos(angle) * inside, np.sin(angle) * inside
    return split_table(np.block([[cosine, -sine], [sine, cosine]]))


def z_forward_table():
    kept = np.concatenate([np.arange(0, 40), np.arange(96, 128)])
    angle = angles(kept, plane_of_holder())
    scale = 1.0 / (WEIGHT * N**3)
    cosine, sine = np.cos(angle) * scale, np.sin(angle) * scale
    return split_table(np.block([[cosine, sine], [-sine, cosine]]))


def box_frequencies(count):
    slot = np.arange(count)
    return slot - CUT, (slot <= 2 * CUT).astype(np.float64)


def y_inverse_table():
    frequency, kept = box_frequencies(LINE)
    angle = angles(frequency, np.arange(N))
    return (np.concatenate([np.cos(angle), np.sin(angle)], 1) * kept[:, None])


def x_inverse_table():
    across = (4 * np.arange(24)[None, :] + np.arange(4)[:, None]).reshape(-1)
    kept = (across <= 2 * CUT).astype(np.float64)
    angle = angles(np.arange(N), across - CUT)
    cosine, sine = WEIGHT * np.cos(angle) * kept, WEIGHT * np.sin(angle) * kept
    return (np.block([[cosine, -sine], [sine, cosine]]))


def x_forward_table():
    frequency, kept = box_frequencies(LINE)
    angle = angles(frequency, np.arange(N))
    cosine, sine = np.cos(angle) * kept[:, None], np.sin(angle) * kept[:, None]
    return (np.block([[cosine, sine], [-sine, cosine]]))


def y_forward_table():
    frequency, kept = box_frequencies(N)
    angle = angles(np.arange(N), frequency)
    return (np.concatenate([np.cos(angle), np.sin(angle)], 1) * np.concatenate([kept, kept])[None, :])


def spread_table():
    table = np.zeros((N, 8, N))
    for band in range(8):
        for part in range(2):
            for eighth in range(8):
                for group in range(4):
                    for half in range(2):
                        table[band * 16 + part * 8 + eighth, eighth, band * 16 + group * 4 + part * 2 + half] = 1.0
    table = table.reshape(N, 4, 2 * N).transpose(1, 0, 2)
    return np.concatenate([table, table], 1).reshape(8 * N, 2 * N)


def real_table():
    row = np.arange(N)
    frequency = np.where(row <= N // 2, row, row - N // 2)
    angle = angles(frequency, np.arange(N))
    values = np.where((row <= N // 2)[:, None], np.cos(angle), np.sin(angle))
    scale = np.where((row == 0) | (row == N // 2), math.sqrt(1.0 / N), math.sqrt(2.0 / N))
    return values * scale[:, None]


def profile_table():
    frequency = np.arange(N) - N // 2
    angle = angles(frequency, np.arange(N))
    return split_table(np.concatenate([np.cos(angle), np.sin(angle)]))


def packed_tables(named, exact={}):
    blocks, places, row = [], {}, 0
    for name, table in named.items():
        parts = split_table(table)
        rows, columns = parts.shape[1:]
        tall = -(-rows // 16) * 16
        block = np.zeros((2, tall, 256), ml_dtypes.bfloat16)
        block[:, :rows, :columns] = parts
        blocks.append(block.reshape(2 * tall, 256))
        places[name] = (row, row + tall, rows, columns)
        row += 2 * tall
    for name, table in exact.items():
        blocks.append(table.astype(ml_dtypes.bfloat16))
        places[name] = row
        row += table.shape[0]
    return np.concatenate(blocks), places


def holder_planes():
    holder = np.arange(N)
    return ((holder % 2) * 8 + holder // 16) * SUBS + (holder // 2) % 8


def early_tables():
    return packed_tables(
        {
            "y_inverse": y_inverse_table(),
            "x_inverse": x_inverse_table(),
            "real": real_table(),
            "real_turned": real_table().T,
        }
    )


def late_tables():
    return packed_tables(
        {
            "real_planes": real_table()[:, holder_planes()],
            "planes_real": real_table().T[holder_planes()],
            "real": real_table(),
            "real_turned": real_table().T,
            "x_forward": x_forward_table(),
            "y_forward": y_forward_table(),
        },
        {"spread": spread_table()},

    )


EARLY, EARLY_PLACES = early_tables()
LATE, LATE_PLACES = late_tables()


def table_of(ref, places, name):
    high, low, rows, columns = places[name]
    return ref[high : high + rows, 0:columns], ref[low : low + rows, 0:columns]


def early_table(ref, name):
    return table_of(ref, EARLY_PLACES, name)


def late_table(ref, name):
    return table_of(ref, LATE_PLACES, name)


def halves(values):
    high = values.astype(bf16)
    return high, (values - high.astype(f32)).astype(bf16)


def dot(a, b, dims=((1,), (0,))):
    return lax.dot_general(a, b, (dims, ((), ())), preferred_element_type=f32)


def dot3(left, right, dims=((1,), (0,))):
    return dot(left[0], right[0], dims) + (dot(left[0], right[1], dims) + dot(left[1], right[0], dims))


def pair(ref):
    return ref[0], ref[1]


def stick_frequencies(columns):
    across = columns >> 7
    inplane = columns & (N - 1)
    across = jnp.where(across >= N // 2, across - N, across)
    inplane = jnp.where(inplane >= N // 2, inplane - N, inplane)
    return across, inplane


def kept_rows(shape):
    row = lax.broadcasted_iota(jnp.int32, shape, 0)
    return jnp.where(row >= 40, row + 56 - N, row)


def sphere_radius(columns):
    across, inplane = stick_frequencies(columns)
    frequency = kept_rows((LINE, columns.shape[1]))
    return frequency * frequency + (across * across + inplane * inplane)


def own_columns(columns_ref):
    group = lax.axis_index(GA_AXES)
    return jnp.concatenate([columns_ref[pl.ds(2 * group + half, 1), :] for half in range(2)], 1)


def lines_kernel(orbital_ref, tangent_ref, columns_ref, table_ref, out_ref):
    inside = sphere_radius(own_columns(columns_ref)) <= CUT * CUT
    for which, ref in enumerate((orbital_ref, tangent_ref)):
        parts = []
        for part in range(2):
            kept = jnp.concatenate([ref[0, part, 0:40, :], ref[0, part, 96:128, :]], 0)
            parts.append(jnp.where(inside, kept, 0.0))
        lines = dot3(pair(table_ref), halves(jnp.concatenate(parts, 0)))
        for part in range(2):
            for half in range(2):
                row = half * 4 + which * 2 + part
                out_ref[pl.ds(row, N, stride=8), :] = lines[part * N : (part + 1) * N, half * N : (half + 1) * N]


def fields_kernel(
    dest_ref,
    lines_ref,
    ions_ref,
    potential_ref,
    core_ref,
    early_ref,
    late_ref,
    fields_ref,
    sums_ref,
    planes_ref,
    late_out,
    turned,
    grid,
    ycos,
    ysin,
    tables,
    arrivals,
):
    own = lax.axis_index(("xl", "yl", "core"))
    copies = [
        pltpu.make_async_copy(early_ref, tables, arrivals.at[0]),
        pltpu.make_async_copy(late_ref, late_out, arrivals.at[1]),
        pltpu.make_async_copy(potential_ref.at[own], planes_ref.at[0], arrivals.at[2]),
        pltpu.make_async_copy(core_ref.at[own], planes_ref.at[1], arrivals.at[3]),
    ]
    for copy in copies:
        copy.start()
    planes_ref[2] = ions_ref[...]
    lower = lax.broadcasted_iota(jnp.int32, (8, N), 0) < 4
    for quad in range(4):
        for half in range(2):
            tiles = []
            for group in range(4 * quad, 4 * quad + 4):
                for sub in range(0, SUBS, 2):
                    first, second = lines_ref[sub * GROUPS + group], lines_ref[(sub + 1) * GROUPS + group]
                    if half == 0:
                        tiles.append(jnp.where(lower, first, pltpu.roll(second, 4, 0)))
                    else:
                        tiles.append(jnp.where(lower, pltpu.roll(first, 4, 0), second))
            base = (quad * 2 + half) * N
            turned[base : base + N, :] = jnp.concatenate(tiles, 0).T
    grid[...] = jnp.zeros_like(grid)
    lane = lax.broadcasted_iota(jnp.int32, (1, N), 1)
    masks = [lane // 32 == slot for slot in range(4)]
    for quad in range(4):

        def scatter(step, carry, quad=quad):
            for inner in range(8):
                stick = step * 8 + inner
                rows = [turned[pl.ds((quad * 2 + half) * N + stick, 1), :] for half in range(2)]
                for slot in range(4):
                    places = dest_ref[(4 * quad + slot) * N + stick]
                    grid[pl.ds(places & 0xFFFF, 1), :] = jnp.where(masks[slot], rows[0], 0.0)
                    grid[pl.ds(places >> 16, 1), :] = jnp.where(masks[slot], rows[1], 0.0)
            return carry

        lax.fori_loop(0, N // 8, scatter, 0)
    lane = lax.broadcasted_iota(jnp.int32, (LINE, N), 1)
    masks = [lane // 32 == slot for slot in range(4)]
    blank = jnp.zeros((N, N), f32)
    for step in range(17, 24):
        ycos[step * PITCH : step * PITCH + N, :] = blank
        ysin[step * PITCH : step * PITCH + N, :] = blank

    copies[0].wait()
    ytable = early_table(tables, "y_inverse")
    for step in range(17):
        packed = None
        for slot in range(4):
            slab = grid[(4 * step + slot) * LINE : (4 * step + slot + 1) * LINE, :]
            slab = slab + pltpu.roll(slab, 64, 1)
            slab = slab + pltpu.roll(slab, 32, 1)
            packed = slab if packed is None else jnp.where(masks[slot], slab, packed)
        lines = dot3(halves(packed.T), ytable)
        ycos[step * PITCH : step * PITCH + N, :] = lines[:, 0:N]
        ysin[step * PITCH : step * PITCH + N, :] = lines[:, N : 2 * N]
    density = jnp.zeros((N, N), f32)
    response = jnp.zeros((N, N), f32)
    xtable = early_table(tables, "x_inverse")
    for band in range(SUBS):
        sides = []
        for which in range(2):
            real, imag = [], []
            for slot in range(4):
                base = slot * 32 + band * 4 + which * 2
                rows = [pl.ds(base + part, 24, stride=PITCH) for part in range(2)]
                real.append(ycos[rows[0], :] - ysin[rows[1], :])
                imag.append(ysin[rows[0], :] + ycos[rows[1], :])
            sides.append(jnp.concatenate(real + imag, 0))
        field = dot3(xtable, halves(jnp.concatenate(sides, 1)))
        fields_ref[band] = field
        first, second = field[:, 0:N], field[:, N : 2 * N]
        density = density + first[0:N] * first[0:N] + first[N : 2 * N] * first[N : 2 * N]
        response = response + first[0:N] * second[0:N] + first[N : 2 * N] * second[N : 2 * N]
    density = density * (1.0 / BANDS)
    response = response * (2.0 / BANDS)
    spectrum = dot3(
        halves(dot3(early_table(tables, "real"), halves(response))), early_table(tables, "real_turned")
    )
    for half in range(2):
        sums_ref[pl.ds(half, 64, stride=4), :] = density[half * 64 : half * 64 + 64]
        sums_ref[pl.ds(2 + half, 64, stride=4), :] = spectrum[half * 64 : half * 64 + 64]
    for copy in copies[1:]:
        copy.wait()


def mix_kernel(arrived_ref, sums_ref, spread_ref):
    for x_low in range(2):
        base = x_low * 128
        rows = [arrived_ref[base + copy * 32 : base + copy * 32 + 32, :] for copy in range(4)]
        sums_ref[x_low * 32 : x_low * 32 + 32, :] = (rows[0] + rows[1]) + (rows[2] + rows[3])
    spectrum = [sums_ref[pl.ds(2 + half, 16, stride=4), :] for half in range(2)]
    for copy in range(8):
        for half in range(2):
            base = copy * 32 + half * 16
            spread_ref[base : base + 16, :] = spectrum[half]


def hartree_kernel(sums_ref, columns_ref, tables_ref, out_ref):
    sides = []
    for half in range(2):
        sides.append(jnp.concatenate([columns_ref[z * 32 + half * 16 : z * 32 + half * 16 + 16, :] for z in range(8)], 0))
    lines = dot3(late_table(tables_ref, "real_planes"), halves(jnp.concatenate(sides, 1)))
    shape = (N, 2 * N)
    row = lax.broadcasted_iota(jnp.int32, shape, 0)
    lane = lax.broadcasted_iota(jnp.int32, shape, 1)
    across = lax.axis_index(BAND_AXES) * 2 + lax.axis_index("xh") + jnp.where(lane >= N, 64, 0)
    inplane = lane & (N - 1)

    def frequency(index):
        return jnp.where(index <= N // 2, index, index - N // 2)

    across, inplane, row = frequency(across), frequency(inplane), frequency(row)
    squares = (row * row + across * across + inplane * inplane).astype(f32)
    kernel = jnp.where(squares == 0.0, 0.0, (4.0 * math.pi / FACTOR) / jnp.where(squares == 0.0, 1.0, squares))
    back = dot3(late_table(tables_ref, "planes_real"), halves(lines * kernel))
    own = lax.axis_index("z")
    mine = back[0:16]
    for z in range(1, 8):
        mine = jnp.where(own == z, back[z * 16 : z * 16 + 16], mine)
    back = mine
    for half in range(2):
        fields = [
            back[:, half * N : (half + 1) * N],
            sums_ref[pl.ds(half, 16, stride=4), :],
            sums_ref[pl.ds(2 + half, 16, stride=4), :],
        ]
        for which, field in enumerate(fields):
            for x_low in range(2):
                for copy in range(4):
                    base = (x_low * 32 + copy * 8) * 6 + which * 2 + half
                    out_ref[pl.ds(base, 8, stride=6), :] = field[x_low * 8 : x_low * 8 + 8]


def own_plane():
    return lax.axis_index(GA_AXES) * SUBS + lax.axis_index(("xl", "yl", "core"))


def ions_kernel(atom_ref, direction_ref, positions_ref, charge_ref, widths_ref, table_ref, out_ref, centres, spreads, marks, charges):
    for slot in range(DISP):
        atom = atom_ref[slot]
        charges[slot : slot + 1, :] = jnp.full((1, N), charge_ref[atom] * (-1.0 / CELL), f32)
        for axis in range(3):
            row = axis * DISP + slot
            centres[row : row + 1, :] = jnp.full((1, N), positions_ref[axis, atom], f32)
            spreads[row : row + 1, :] = jnp.full((1, N), widths_ref[atom], f32)
            marks[row : row + 1, :] = jnp.full((1, N), jnp.where(direction_ref[slot] == axis, 1.0, 0.0), f32)
    frequency = lax.broadcasted_iota(jnp.int32, (3 * DISP, N), 1) - N // 2
    wavenum = frequency.astype(f32) * (2.0 * math.pi / CELL)
    damping = jnp.exp(-0.5 * (wavenum * spreads[...]) ** 2)
    phase = wavenum * centres[...]
    cosine, sine = damping * jnp.cos(phase), damping * jnp.sin(phase)
    chosen = marks[...] > 0.5
    with_cos = jnp.where(chosen, -wavenum * sine, cosine)
    with_sin = jnp.where(chosen, wavenum * cosine, sine)
    profiles = dot3(halves(jnp.concatenate([with_cos, with_sin], 1)), pair(table_ref))
    along_x, along_y, along_z = profiles[0:8], profiles[8:16], profiles[16:24]
    lane = lax.broadcasted_iota(jnp.int32, (DISP, N), 1)
    here = jnp.sum(jnp.where(lane == own_plane(), along_z, 0.0), 1, keepdims=True)
    scaled = along_y * here * charges[...]
    padding = jnp.zeros((N - DISP, N), f32)
    left = jnp.concatenate([along_x, padding], 0).T
    right = jnp.concatenate([scaled, padding], 0)
    out_ref[...] = dot3(halves(left), halves(right))


def products_kernel(
    dest_ref,
    fields_ref,
    solved_ref,
    planes_ref,
    tables_ref,
    out_ref,
    lines,
    grid,
    gathered,
):
    def solved(which):
        return jnp.concatenate([solved_ref[pl.ds(which * 2 + half, 64, stride=6), :] for half in range(2)], 0)

    waves = dot3(late_table(tables_ref, "real_turned"), halves(jnp.concatenate([solved(0), solved(2)], 1)))
    waves = dot3(halves(jnp.concatenate([waves[:, 0:N], waves[:, N : 2 * N]], 0)), late_table(tables_ref, "real"))
    hartree, response = waves[0:N], waves[N : 2 * N]
    total = solved(1) + planes_ref[1]
    root = jnp.exp(jnp.log(total) * (1.0 / 3.0))
    exchange = -SLATER * root
    effective = planes_ref[0] + exchange
    change = exchange / (3.0 * total) * response + hartree + planes_ref[2]
    xtable = late_table(tables_ref, "x_forward")
    ytable = late_table(tables_ref, "y_forward")
    effective2 = jnp.concatenate([effective, effective], 0)
    change2 = jnp.concatenate([change, change], 0)
    blocks = [[], []]
    for couple in range(SUBS // 2):
        sides = []
        for band in (2 * couple, 2 * couple + 1):
            sides.append(effective2 * fields_ref[band, :, N : 2 * N] + change2 * fields_ref[band, :, 0:N])
        across = dot3(xtable, halves(jnp.concatenate(sides, 1)))
        rows = jnp.concatenate([across[:, 0:N], across[:, N : 2 * N]], 0)
        done = dot3(halves(rows), ytable)
        for side in range(2):
            real = done[side * 144 : side * 144 + 72]
            imag = done[side * 144 + 72 : side * 144 + 144]
            base = (2 * couple + side) * 144
            lines[base : base + 72, :] = real[:, 0:N] + imag[:, N : 2 * N]
            lines[base + 72 : base + 144, :] = imag[:, 0:N] - real[:, N : 2 * N]
    first = LATE_PLACES["spread"]
    spread = [tables_ref[first + block * 2 * N : first + (block + 1) * 2 * N, :] for block in range(4)]
    for eight in range(9):
        tiles = [lines[half * 72 + eight * 8 : half * 72 + eight * 8 + 8, :] for half in range(16)]
        turned = jnp.concatenate(tiles, 0).T[0:LINE]
        high, low = halves(turned)
        both = jnp.concatenate([high, low], 1)
        for block in range(4):
            cells = dot(both, spread[block])
            for side in range(2):
                base = (eight * 8 + block * 2 + side) * LINE
                grid[base : base + LINE, :] = cells[:, side * N : (side + 1) * N]
    lane = lax.broadcasted_iota(jnp.int32, (1, N), 1)
    slot_of_lane = ((lane // 4) % 4) * 2 + lane % 2
    masks = [slot_of_lane == slot for slot in range(1, 8)]
    for block in range(4):

        def gather(step, carry, block=block):
            for inner in range(8):
                stick = step * 8 + inner
                row = None
                for slot in range(4):
                    places = dest_ref[(4 * block + slot) * N + stick]
                    cells = [grid[pl.ds(places & 0xFFFF, 1), :], grid[pl.ds(places >> 16, 1), :]]
                    for half in range(2):
                        row = cells[half] if row is None else jnp.where(masks[2 * slot + half - 1], cells[half], row)
                gathered[pl.ds(stick, 1), :] = row
            return carry

        lax.fori_loop(0, N // 8, gather, 0)
        turned = gathered[...].T
        for band in range(SUBS):
            base = band * 64 + block * 16
            out_ref[base : base + 16, :] = turned[band * 16 : band * 16 + 16]


def result_kernel(arrived_ref, tangent_ref, columns_ref, table_ref, out_ref):
    sides = []
    for half in range(2):
        parts = [arrived_ref[pl.ds(part * 2 + half, N, stride=4), :] for part in range(2)]
        sides.append(jnp.concatenate(parts, 0))
    lines = dot3(pair(table_ref), halves(jnp.concatenate(sides, 1)))
    radius = sphere_radius(own_columns(columns_ref))
    inside = radius <= CUT * CUT
    kinetic = (0.5 * FACTOR) * radius.astype(f32)
    for part in range(2):
        kept = jnp.concatenate([tangent_ref[0, part, 0:40, :], tangent_ref[0, part, 96:128, :]], 0)
        rows = jnp.where(inside, lines[part * LINE : (part + 1) * LINE] + kinetic * kept, 0.0)
        out_ref[0, part, 0:40, :] = rows[0:40]
        out_ref[0, part, 40:96, :] = jnp.zeros((56, 256), f32)
        out_ref[0, part, 96:128, :] = rows[40:72]


def vmem(count):
    return [pl.BlockSpec(memory_space=pltpu.VMEM)] * count


def anywhere(count):
    return [pl.BlockSpec(memory_space=pltpu.HBM)] * count


def smem(count):
    return [pl.BlockSpec(memory_space=pltpu.SMEM)] * count


def shape(*dims):
    return jax.ShapeDtypeStruct(dims, f32)


def call(kernel, out_shape, in_specs, mebibytes, scratch=()):
    several = isinstance(out_shape, tuple)
    return pl.pallas_call(
        kernel,
        out_shape=out_shape,
        in_specs=in_specs,
        out_specs=tuple(vmem(len(out_shape))) if several else vmem(1)[0],
        scratch_shapes=scratch,
        compiler_params=pltpu.CompilerParams(vmem_limit_bytes=(mebibytes << 20) or None),
        name=kernel.__name__.removesuffix("_kernel"),
    )


def exchange(values, axes):
    return lax.all_to_all(values, axes, 0, 0, tiled=True)


def body(
    orbitals,
    orbital_tangent,
    stick_columns,
    ion_potential,
    core_density,
    positions,
    z_charge,
    widths,
    atom_index,
    direction,
):
    columns = stick_columns.reshape(STICKS // N, N)
    across, inplane = stick_frequencies(stick_columns)
    cell = (across + CUT) * LINE + (inplane + CUT)
    dest = jnp.where(across * across + inplane * inplane <= CUT * CUT, cell, DUMP).reshape(GROUPS, 2, N)
    dest = (dest[:, 0] + dest[:, 1] * 65536).reshape(-1)
    lines = call(lines_kernel, shape(N * 8, N), vmem(4), 0)(orbitals, orbital_tangent, columns, z_inverse_table())
    lines = exchange(lines.reshape(N, 8, N), PLANE_AXES)
    ions = call(
        ions_kernel, shape(N, N), smem(5) + vmem(1), 4, [pltpu.VMEM((24, N), f32)] * 3 + [pltpu.VMEM((8, N), f32)]
    )(atom_index, direction, positions.T, z_charge, widths, profile_table())
    fields, sums, planes, tables = call(
        fields_kernel,
        (
            shape(SUBS, 2 * N, 2 * N),
            shape(2 * N, N),
            shape(3, N, N),
            jax.ShapeDtypeStruct(LATE.shape, bf16),
        ),
        smem(1) + vmem(2) + anywhere(4),
        24,
        [
            pltpu.VMEM((8 * N, N), f32),
            pltpu.VMEM((CELLS, N), f32),
            pltpu.VMEM((24 * PITCH, N), f32),
            pltpu.VMEM((24 * PITCH, N), f32),
            pltpu.VMEM(EARLY.shape, bf16),
            pltpu.SemaphoreType.DMA((4,)),
        ],
    )(dest, lines, ions, ion_potential, core_density, EARLY, LATE)
    sums = exchange(sums.reshape(64, 4, N), BAND_AXES + ("xh",)).reshape(2 * N, N)
    sums, spectrum = call(mix_kernel, (shape(64, N), shape(2 * N, N)), vmem(1), 4)(sums)
    spectrum = exchange(spectrum.reshape(8, 32, N), "z").reshape(2 * N, N)
    solved = call(hartree_kernel, shape(3 * N, N), vmem(3), 4)(sums, spectrum, tables)
    solved = exchange(solved.reshape(64, 3, 2, N), BAND_AXES + ("xh",)).reshape(3 * N, N)
    outgoing = call(
        products_kernel,
        shape(4 * N, N),
        smem(1) + vmem(4),
        20,
        [
            pltpu.VMEM((16 * LINE, N), f32),
            pltpu.VMEM((LINE * LINE, N), f32),
            pltpu.VMEM((N, N), f32),
        ],
    )(
        dest,
        fields,
        solved,
        planes,
        tables,
    )
    arrived = exchange(outgoing.reshape(N, 4, N), PLANE_AXES).reshape(4 * N, N)
    return call(result_kernel, shape(1, 2, N, 256), vmem(4), 8)(arrived, orbital_tangent, columns, z_forward_table())


def solution(mesh):
    fine = Mesh(mesh.devices.reshape(2, 4, 2, 2, 2, 8), BAND_AXES + GA_AXES)
    lines = P(BAND_AXES, None, None, GA_AXES)
    planes = P(GA_AXES, None, None)
    return jax.shard_map(
        body,
        mesh=fine,
        in_specs=(lines, lines, P(), planes, planes, P(), P(), P(), P(), P()),
        out_specs=lines,
        check_vma=False,
    )
```

time: 146 us -> 123 us (0.84)
  local copies, waits for them, and re-layouts: 12.1 us -> 1.09 us
  starting transfers between devices: 27.2 us -> 16.6 us
  blocking collectives: 58.7 us -> 65.7 us
  Pallas kernels: 26.8 us -> 21.6 us
  waiting for transfers between devices: 19.4 us -> 17.2 us
    all_to_all x2 -> x4, blocking collectives: 41.9 us -> 65.7 us  [exchange(): return lax.all_to_all(values, axes, 0, 0, tiled=True)]
    all_gather x1 -> x0, blocking collectives: 16.9 us -> none  [body(): sums = lax.all_gather(sums, 'yh')]
    all_to_all x3 -> x1, starting transfers between devices: 27.2 us -> 16.6 us  [exchange(): return lax.all_to_all(values, axes, 0, 0, tiled=True)]
    pallas_call x6 -> x7, Pallas kernels: 26.8 us -> 21.6 us  [the longest x1 8.7 us: body(): call(fields_kernel, (shape(SUBS, 2 * N, 2 * N), shape(2 * N, N), shape(3,...]
    unnamed x29 -> x26, local copies, waits for them, and re-layouts: 5.41 us -> 1.09 us
    dynamic_slice x3 -> x0, local copies, waits for them, and re-layouts: 3.53 us -> none  [the longest x1 1.38 us: body(): lax.dynamic_slice_in_dim(stick_columns, group * 256, 256).reshape(1, 256)]
    reshape x1 -> x0, local copies, waits for them, and re-layouts: 2.47 us -> none  [body(): positions.reshape(-1)]
    all_to_all x3 -> x1, waiting for transfers between devices: 19.4 us -> 17.2 us  [exchange(): return lax.all_to_all(values, axes, 0, 0, tiled=True)]
  transfers between devices with their start and end apart: 3 -> 1, of which waited for: 2 -> 1; matrix products, arithmetic and copies ran while one was open for 5% -> 0% of each run, Pallas kernels for 2% -> 2%
where the time goes in v1:
time: 123 us
  blocking collectives  65.7 us (53%)
  Pallas kernels  21.6 us (18%)
  waiting for transfers between devices  17.2 us (14%)
  starting transfers between devices  16.6 us (13%)
    all_to_all x4, blocking collectives, exchange(): return lax.all_to_all(values, axes, 0, 0, tiled=True)  65.7 us
    all_to_all x1, waiting for transfers between devices, exchange(): return lax.all_to_all(values, axes, 0, 0, tiled=True)  17.2 us
    all_to_all x1, starting transfers between devices, exchange(): return lax.all_to_all(values, axes, 0, 0, tiled=True)  16.6 us
    pallas_call x1, Pallas kernels, body(): call(fields_kernel, (shape(SUBS, 2 * N, 2 * N), shape(2 * N, N), shape(3,...  8.7 us
    pallas_call x1, Pallas kernels, body(): call(products_kernel, shape(4 * N, N), smem(1) + vmem(4), 20, [pltpu.VMEM...  7.2 us
    pallas_call x1, Pallas kernels, body(): call(lines_kernel, shape(N * 8, N), vmem(4), 0)  2.46 us
  transfers between devices with their start and end apart: 1, of which 1 were waited for; matrix products, arithmetic and copies ran while one was open for 0% of the time, Pallas kernels for 2%

profile of v1, /device:TPU:1, one launch (start us, length us, event | category | flops | bytes accessed | tf_op | source)
XLA Modules:
  0.0 122.5 jit_solution(14994226842004627453)
XLA Ops:
  0.0 0.0 copy-start.7
  0.0 0.0 copy-start.6
  0.0 0.0 copy-start.12
  0.0 0.0 copy-start.11
  0.0 0.0 copy-start.10
  0.0 0.0 copy-start.9
  0.0 0.0 copy-start.8
  0.0 0.0 copy-start
  0.1 0.0 copy-start.2
  0.1 0.0 copy-start.3
  0.1 2.5 %lines.1 = f32[1024,128]{1,0:T(8,128)} custom-call(f32[1,2,128,256]{3,2,1,0:T(8,128)} %orbital_ref.1, f32[1,2,128,256]{3,2,1,0:T(8,128)} %tangent_ref.3, s32[32,128]{1,0:T(8,128)} %bitcast.19, bf16[2,256,144]{2,1,0:T(8,128)(2,1)} %constant.30.clone.table_ref), custom_call_target="tpu_custom_call" | custom-call | tf_op jit(solution)/shard_map/lines/pallas_call | solution.py:584
  2.5 16.6 %all-to-all-start = ((f32[128,8,128]{2,1,0:T(8,128)}), f32[128,8,128]{2,1,0:T(8,128)S(1)}, u32[]{:S(2)}, u32[]{:S(2)}) async-start(f32[128,8,128]{2,1,0:T(8,128)} %bitcast.26), calls=%async_computation | async-start | bytes 1048576 | tf_op jit(solution)/shard_map/all_to_all | solution.py:564
  19.2 0.0 copy-done.7
  19.2 0.0 copy-done.12
  19.2 0.0 copy-done.11
  19.2 0.0 copy-done.10
  19.2 0.0 copy-done.9
  19.2 0.0 copy-done.8
  19.3 1.9 %ions.1.ions_ref = f32[128,128]{1,0:T(8,128)S(1)} custom-call(s32[8]{0:T(128)S(1)} %copy-done.11, s32[8]{0:T(128)S(1)} %copy-done.12, f32[3,2000]{1,0:T(4,128)S(1)} %bitcast.25, f32[2000]{0:T(1024)S(1)} %copy-done.9, f32[2000]{0:T(1024)S(1)} %copy-done.10, bf16[2,256,128]{2,1,0:T(8,128)(2,1)S(1)} %copy-done.7), custom_call_target="tpu_custom_call" | custom-call | tf_op jit(solution)/shard_map/ions/pallas_call | solution.py:586
  21.2 0.0 copy-done.6
  21.2 17.2 %all-to-all-done.lines_ref = f32[128,8,128]{2,1,0:T(8,128)S(1)} async-done(((f32[128,8,128]{2,1,0:T(8,128)}), f32[128,8,128]{2,1,0:T(8,128)S(1)}, u32[]{:S(2)}, u32[]{:S(2)}) %all-to-all-start) | async-done | bytes 524320 | tf_op jit(solution)/shard_map/all_to_all | solution.py:564
  38.4 0.0 copy-done
  38.5 0.0 copy-done.2
  38.5 0.0 copy-done.3
  38.5 0.0 copy-start.4
  38.5 1.0 copy-done.4
  39.5 8.7 %fields.1 = (f32[8,256,256]{2,1,0:T(8,128)S(1)}, f32[256,128]{1,0:T(8,128)S(1)}, f32[3,128,128]{2,1,0:T(8,128)S(1)}, bf16[2592,256]{1,0:T(8,128)(2,1)S(1)}) custom-call(s32[2048]{0:T(1024)S(1)} %bitcast.23, f32[128,8,128]{2,1,0:T(8,128)S(1)} %all-to-all-done.lines_ref, f32[128,128]{1,0:T(8,128)S(1)} %ions.1.ions_ref, f32[8,128,128]{2,1,0:T(8,128)S(1)} %copy-done.3, ...), custom_call_target="tpu_custom_call" | custom-call | tf_op jit(solution)/shard_map/fields/pallas_call | solution.py:589
  48.2 19.3 %all_to_all.25 = f32[64,4,128]{2,1,0:T(4,128)S(1)} all-to-all(f32[64,4,128]{2,1,0:T(4,128)S(1)} %bitcast.21), channel_id=1, replica_groups=mesh['xl'=2,'yh'=4,'yl'=2,'core'=2,'xh'=2,'z'=8] {'xl','yh','yl','core',..., dimensions={0} | all-to-all | bytes 262144 | tf_op jit(solution)/shard_map/all_to_all | solution.py:564
  67.5 10.8 %all_to_all.26 = f32[8,32,128]{2,1,0:T(8,128)S(1)} all-to-all(f32[8,32,128]{2,1,0:T(8,128)S(1)} %bitcast.22), channel_id=1, replica_groups=mesh['xl'=2,'yh'=4,'yl'=2,'core'=2,'xh'=2,'z'=8] {'z'}, dimensions={0} | all-to-all | bytes 262144 | tf_op jit(solution)/shard_map/all_to_all | solution.py:564
  78.3 0.4 hartree.1
  78.7 17.2 %all_to_all.27 = f32[64,3,2,128]{3,2,1,0:T(2,128)S(1)} all-to-all(f32[64,3,2,128]{3,2,1,0:T(2,128)S(1)} %bitcast.16), channel_id=1, replica_groups=mesh['xl'=2,'yh'=4,'yl'=2,'core'=2,'xh'=2,'z'=8] {'xl','yh','yl','core',..., dimensions={0} | all-to-all | bytes 393216 | tf_op jit(solution)/shard_map/all_to_all | solution.py:564
  95.9 0.0 copy-start.1
  95.9 0.0 copy-start.5
  95.9 7.2 %products.1 = f32[512,128]{1,0:T(8,128)S(1)} custom-call(s32[2048]{0:T(1024)S(1)} %bitcast.24, f32[8,256,256]{2,1,0:T(8,128)S(1)} %get-tuple-element.11.fields_ref, f32[384,128]{1,0:T(8,128)S(1)} %bitcast.15, f32[3,128,128]{2,1,0:T(8,128)S(1)} %get-tuple-element.16.planes_ref, bf16[2592,256]{1,0:T(8,128)(2,1)S(1)} %get-tuple-element.15.tables_ref), custom_call_target="tpu_custom_call" | custom-call | tf_op jit(solution)/shard_map/products/pallas_call | solution.py:613
  103.1 18.5 %all_to_all.28 = f32[128,4,128]{2,1,0:T(4,128)S(1)} all-to-all(f32[128,4,128]{2,1,0:T(4,128)S(1)} %bitcast.13), channel_id=1, replica_groups=mesh['xl'=2,'yh'=4,'yl'=2,'core'=2,'xh'=2,'z'=8] {'xl','yl','core','xh',..., dimensions={0} | all-to-all | bytes 524288 | tf_op jit(solution)/shard_map/all_to_all | solution.py:564
  121.6 0.0 copy-done.1
  121.6 0.0 copy-done.5
  121.6 0.9 result.1
  (3 shorter events, 0.0 us)
Async XLA Ops:
  0.0 19.2 %copy-start.7 = (bf16[2,256,128]{2,1,0:T(8,128)(2,1)S(1)}, bf16[2,256,128]{2,1,0:T(8,128)(2,1)}, u32[]{:S(2)}) copy-start(bf16[2,256,128]{2,1,0:T(8,128)(2,1)} %constant.31.clone.table_ref) | copy-start | bytes 393220
  0.0 21.2 %copy-start.6 = (s32[4096]{0:T(1024)S(1)}, s32[4096]{0:T(1024)}, u32[]{:S(2)}) copy-start(s32[4096]{0:T(1024)} %param.17) | copy-start | bytes 49156
  0.0 19.2 %copy-start.12 = (s32[8]{0:T(128)S(1)}, s32[8]{0:T(128)}, u32[]{:S(2)}) copy-start(s32[8]{0:T(128)} %direction_ref.1) | copy-start | bytes 100
  0.0 19.2 %copy-start.11 = (s32[8]{0:T(128)S(1)}, s32[8]{0:T(128)}, u32[]{:S(2)}) copy-start(s32[8]{0:T(128)} %atom_ref.1) | copy-start | bytes 100
  0.0 19.2 %copy-start.10 = (f32[2000]{0:T(1024)S(1)}, f32[2000]{0:T(1024)}, u32[]{:S(2)}) copy-start(f32[2000]{0:T(1024)} %widths_ref.1) | copy-start | bytes 24004
  0.0 19.2 %copy-start.9 = (f32[2000]{0:T(1024)S(1)}, f32[2000]{0:T(1024)}, u32[]{:S(2)}) copy-start(f32[2000]{0:T(1024)} %charge_ref.1) | copy-start | bytes 24004
  0.0 19.2 %copy-start.8 = (f32[2000,3]{0,1:T(4,128)S(1)}, f32[2000,3]{0,1:T(4,128)}, u32[]{:S(2)}) copy-start(f32[2000,3]{0,1:T(4,128)} %param.20) | copy-start | bytes 72004
  0.0 38.4 %copy-start = (bf16[2592,256]{1,0:T(8,128)(2,1)S(1)}, bf16[2592,256]{1,0:T(8,128)(2,1)}, u32[]{:S(2)}) copy-start(bf16[2592,256]{1,0:T(8,128)(2,1)} %constant.33.clone.late_ref) | copy-start | bytes 3981316
  0.1 38.4 %copy-start.2 = (bf16[1184,256]{1,0:T(8,128)(2,1)S(1)}, bf16[1184,256]{1,0:T(8,128)(2,1)}, u32[]{:S(2)}) copy-start(bf16[1184,256]{1,0:T(8,128)(2,1)} %constant.32.clone.early_ref) | copy-start | bytes 1818628
  0.1 38.4 %copy-start.3 = (f32[8,128,128]{2,1,0:T(8,128)S(1)}, f32[8,128,128]{2,1,0:T(8,128)}, u32[]{:S(2)}) copy-start(f32[8,128,128]{2,1,0:T(8,128)} %potential_ref.1) | copy-start | bytes 1572868
  2.5 35.9 %all-to-all-start = ((f32[128,8,128]{2,1,0:T(8,128)}), f32[128,8,128]{2,1,0:T(8,128)S(1)}, u32[]{:S(2)}, u32[]{:S(2)}) async-start(f32[128,8,128]{2,1,0:T(8,128)} %bitcast.26), calls=%async_computation | async-start | bytes 1048576 | tf_op jit(solution)/shard_map/all_to_all | solution.py:564
  38.5 1.0 copy-start.4
  95.9 25.7 %copy-start.1 = (f32[1,2,128,256]{3,2,1,0:T(8,128)S(1)}, f32[1,2,128,256]{3,2,1,0:T(8,128)}, u32[]{:S(2)}) copy-start(f32[1,2,128,256]{3,2,1,0:T(8,128)} %tangent_ref.3) | copy-start | bytes 786436
  95.9 25.7 %copy-start.5 = (bf16[2,144,256]{2,1,0:T(8,128)(2,1)S(1)}, bf16[2,144,256]{2,1,0:T(8,128)(2,1)}, u32[]{:S(2)}) copy-start(bf16[2,144,256]{2,1,0:T(8,128)(2,1)} %constant.34.clone.table_ref) | copy-start | bytes 442372

commit v2 on v1

--- a/solution.py
+++ b/solution.py
@@ -113,6 +113,16 @@
                         table[band * 16 + part * 8 + eighth, eighth, band * 16 + group * 4 + part * 2 + half] = 1.0
     table = table.reshape(N, 4, 2 * N).transpose(1, 0, 2)
     return np.concatenate([table, table], 1).reshape(8 * N, 2 * N)
+
+
+def replicate_table():
+    table = np.zeros((N, 4, 4, 2, 16))
+    for group in range(4):
+        for part in range(2):
+            for entry in range(16):
+                table[group * 32 + entry * 2 + part, group, :, part, entry] = 1.0
+    table = table.reshape(N, 2, 2 * N).transpose(1, 0, 2)
+    return np.concatenate([table, table], 1).reshape(4 * N, 2 * N)
 
 
 def real_table():
@@ -160,7 +170,8 @@
             "x_inverse": x_inverse_table(),
             "real": real_table(),
             "real_turned": real_table().T,
-        }
+        },
+        {"replicate": replicate_table()},
     )
 
 
@@ -251,35 +262,18 @@
                 out_ref[pl.ds(row, N, stride=8), :] = lines[part * N : (part + 1) * N, half * N : (half + 1) * N]
 
 
+def circle_reach(slot):
+    across = slot - CUT
+    return math.isqrt(CUT * CUT - across * across) if abs(across) <= CUT else -1
+
+
 def fields_kernel(
-    dest_ref,
-    lines_ref,
-    ions_ref,
-    potential_ref,
-    core_ref,
-    early_ref,
-    late_ref,
-    fields_ref,
-    sums_ref,
-    planes_ref,
-    late_out,
-    turned,
-    grid,
-    ycos,
-    ysin,
-    tables,
-    arrivals,
+    dest_ref, lines_ref, planes_ref, tables, late_ref, fields_ref, sums_ref, late_out, turned, grid, middle, arrival
 ):
-    own = lax.axis_index(("xl", "yl", "core"))
-    copies = [
-        pltpu.make_async_copy(early_ref, tables, arrivals.at[0]),
-        pltpu.make_async_copy(late_ref, late_out, arrivals.at[1]),
-        pltpu.make_async_copy(potential_ref.at[own], planes_ref.at[0], arrivals.at[2]),
-        pltpu.make_async_copy(core_ref.at[own], planes_ref.at[1], arrivals.at[3]),
-    ]
-    for copy in copies:
-        copy.start()
-    planes_ref[2] = ions_ref[...]
+    del planes_ref
+    copy = pltpu.make_async_copy(late_ref, late_out, arrival)
+    copy.start()
+    replicate = tables[EARLY_PLACES["replicate"] : EARLY_PLACES["replicate"] + 4 * N, :]
     lower = lax.broadcasted_iota(jnp.int32, (8, N), 0) < 4
     for quad in range(4):
         for half in range(2):
@@ -291,56 +285,56 @@
                         tiles.append(jnp.where(lower, first, pltpu.roll(second, 4, 0)))
                     else:
                         tiles.append(jnp.where(lower, pltpu.roll(first, 4, 0), second))
+            both = jnp.concatenate(halves(jnp.concatenate(tiles, 0).T), 1)
             base = (quad * 2 + half) * N
-            turned[base : base + N, :] = jnp.concatenate(tiles, 0).T
-    grid[...] = jnp.zeros_like(grid)
-    lane = lax.broadcasted_iota(jnp.int32, (1, N), 1)
-    masks = [lane // 32 == slot for slot in range(4)]
+            for couple in range(2):
+                copies = dot(both, replicate[couple * 2 * N : (couple + 1) * 2 * N])
+                for side in range(2):
+                    turned[2 * couple + side, base : base + N, :] = copies[:, side * N : (side + 1) * N]
     for quad in range(4):
 
         def scatter(step, carry, quad=quad):
             for inner in range(8):
                 stick = step * 8 + inner
-                rows = [turned[pl.ds((quad * 2 + half) * N + stick, 1), :] for half in range(2)]
                 for slot in range(4):
                     places = dest_ref[(4 * quad + slot) * N + stick]
-                    grid[pl.ds(places & 0xFFFF, 1), :] = jnp.where(masks[slot], rows[0], 0.0)
-                    grid[pl.ds(places >> 16, 1), :] = jnp.where(masks[slot], rows[1], 0.0)
+                    grid[pl.ds(places & 0xFFFF, 1), :] = turned[slot, pl.ds(quad * 2 * N + stick, 1), :]
+                    grid[pl.ds(places >> 16, 1), :] = turned[slot, pl.ds((quad * 2 + 1) * N + stick, 1), :]
             return carry
 
         lax.fori_loop(0, N // 8, scatter, 0)
     lane = lax.broadcasted_iota(jnp.int32, (LINE, N), 1)
+    distance = jnp.abs(lax.broadcasted_iota(jnp.int32, (LINE, N), 0) - CUT)
     masks = [lane // 32 == slot for slot in range(4)]
-    blank = jnp.zeros((N, N), f32)
     for step in range(17, 24):
-        ycos[step * PITCH : step * PITCH + N, :] = blank
-        ysin[step * PITCH : step * PITCH + N, :] = blank
-
-    copies[0].wait()
+        middle[step * PITCH : step * PITCH + N, :] = jnp.zeros((N, N), f32)
     ytable = early_table(tables, "y_inverse")
     for step in range(17):
         packed = None
         for slot in range(4):
             slab = grid[(4 * step + slot) * LINE : (4 * step + slot + 1) * LINE, :]
-            slab = slab + pltpu.roll(slab, 64, 1)
-            slab = slab + pltpu.roll(slab, 32, 1)
             packed = slab if packed is None else jnp.where(masks[slot], slab, packed)
+        reach = jnp.full((1, N), circle_reach(4 * step), jnp.int32)
+        for slot in range(1, 4):
+            reach = jnp.where(masks[slot][0:1], circle_reach(4 * step + slot), reach)
+        packed = jnp.where(distance <= reach, packed, 0.0)
         lines = dot3(halves(packed.T), ytable)
-        ycos[step * PITCH : step * PITCH + N, :] = lines[:, 0:N]
-        ysin[step * PITCH : step * PITCH + N, :] = lines[:, N : 2 * N]
+        for slot in range(4):
+            real, imag = lines[slot * 32 : slot * 32 + 16], lines[slot * 32 + 16 : slot * 32 + 32]
+            base = step * PITCH + slot * 16
+            middle[base : base + 16, :] = real[:, 0:N] - imag[:, N : 2 * N]
+            middle[base + 64 : base + 80, :] = real[:, N : 2 * N] + imag[:, 0:N]
     density = jnp.zeros((N, N), f32)
     response = jnp.zeros((N, N), f32)
     xtable = early_table(tables, "x_inverse")
     for band in range(SUBS):
         sides = []
         for which in range(2):
-            real, imag = [], []
-            for slot in range(4):
-                base = slot * 32 + band * 4 + which * 2
-                rows = [pl.ds(base + part, 24, stride=PITCH) for part in range(2)]
-                real.append(ycos[rows[0], :] - ysin[rows[1], :])
-                imag.append(ysin[rows[0], :] + ycos[rows[1], :])
-            sides.append(jnp.concatenate(real + imag, 0))
+            rows = []
+            for part in range(2):
+                for slot in range(4):
+                    rows.append(middle[pl.ds(part * 64 + slot * 16 + band * 2 + which, 24, stride=PITCH), :])
+            sides.append(jnp.concatenate(rows, 0))
         field = dot3(xtable, halves(jnp.concatenate(sides, 1)))
         fields_ref[band] = field
         first, second = field[:, 0:N], field[:, N : 2 * N]
@@ -354,8 +348,7 @@
     for half in range(2):
         sums_ref[pl.ds(half, 64, stride=4), :] = density[half * 64 : half * 64 + 64]
         sums_ref[pl.ds(2 + half, 64, stride=4), :] = spectrum[half * 64 : half * 64 + 64]
-    for copy in copies[1:]:
-        copy.wait()
+    copy.wait()
 
 
 def mix_kernel(arrived_ref, sums_ref, spread_ref):
@@ -410,7 +403,29 @@
     return lax.axis_index(GA_AXES) * SUBS + lax.axis_index(("xl", "yl", "core"))
 
 
-def ions_kernel(atom_ref, direction_ref, positions_ref, charge_ref, widths_ref, table_ref, out_ref, centres, spreads, marks, charges):
+def ions_kernel(
+    atom_ref,
+    direction_ref,
+    positions_ref,
+    charge_ref,
+    widths_ref,
+    table_ref,
+    potential_ref,
+    core_ref,
+    out_ref,
+    centres,
+    spreads,
+    marks,
+    charges,
+    arrivals,
+):
+    own = lax.axis_index(("xl", "yl", "core"))
+    copies = [
+        pltpu.make_async_copy(potential_ref.at[own], out_ref.at[0], arrivals.at[0]),
+        pltpu.make_async_copy(core_ref.at[own], out_ref.at[1], arrivals.at[1]),
+    ]
+    for copy in copies:
+        copy.start()
     for slot in range(DISP):
         atom = atom_ref[slot]
         charges[slot : slot + 1, :] = jnp.full((1, N), charge_ref[atom] * (-1.0 / CELL), f32)
@@ -435,7 +450,9 @@
     padding = jnp.zeros((N - DISP, N), f32)
     left = jnp.concatenate([along_x, padding], 0).T
     right = jnp.concatenate([scaled, padding], 0)
-    out_ref[...] = dot3(halves(left), halves(right))
+    out_ref[2] = dot3(halves(left), halves(right))
+    for copy in copies:
+        copy.wait()
 
 
 def products_kernel(
@@ -583,28 +600,25 @@
     dest = (dest[:, 0] + dest[:, 1] * 65536).reshape(-1)
     lines = call(lines_kernel, shape(N * 8, N), vmem(4), 0)(orbitals, orbital_tangent, columns, z_inverse_table())
     lines = exchange(lines.reshape(N, 8, N), PLANE_AXES)
-    ions = call(
-        ions_kernel, shape(N, N), smem(5) + vmem(1), 4, [pltpu.VMEM((24, N), f32)] * 3 + [pltpu.VMEM((8, N), f32)]
-    )(atom_index, direction, positions.T, z_charge, widths, profile_table())
-    fields, sums, planes, tables = call(
+    planes = call(
+        ions_kernel,
+        shape(3, N, N),
+        smem(5) + vmem(1) + anywhere(2),
+        4,
+        [pltpu.VMEM((24, N), f32)] * 3 + [pltpu.VMEM((8, N), f32), pltpu.SemaphoreType.DMA((2,))],
+    )(atom_index, direction, positions.T, z_charge, widths, profile_table(), ion_potential, core_density)
+    fields, sums, tables = call(
         fields_kernel,
-        (
-            shape(SUBS, 2 * N, 2 * N),
-            shape(2 * N, N),
-            shape(3, N, N),
-            jax.ShapeDtypeStruct(LATE.shape, bf16),
-        ),
-        smem(1) + vmem(2) + anywhere(4),
+        (shape(SUBS, 2 * N, 2 * N), shape(2 * N, N), jax.ShapeDtypeStruct(LATE.shape, bf16)),
+        smem(1) + vmem(1) + anywhere(1) + vmem(1) + anywhere(1),
         24,
         [
-            pltpu.VMEM((8 * N, N), f32),
+            pltpu.VMEM((4, 8 * N, N), f32),
             pltpu.VMEM((CELLS, N), f32),
             pltpu.VMEM((24 * PITCH, N), f32),
-            pltpu.VMEM((24 * PITCH, N), f32),
-            pltpu.VMEM(EARLY.shape, bf16),
-            pltpu.SemaphoreType.DMA((4,)),
+            pltpu.SemaphoreType.DMA,
         ],
-    )(dest, lines, ions, ion_potential, core_density, EARLY, LATE)
+    )(dest, lines, planes, EARLY, LATE)
     sums = exchange(sums.reshape(64, 4, N), BAND_AXES + ("xh",)).reshape(2 * N, N)
     sums, spectrum = call(mix_kernel, (shape(64, N), shape(2 * N, N)), vmem(1), 4)(sums)
     spectrum = exchange(spectrum.reshape(8, 32, N), "z").reshape(2 * N, N)

time: 123 us -> 121 us (0.984)
  waiting for transfers between devices: 17.2 us -> 15.1 us
    all_to_all x1, waiting for transfers between devices: 17.2 us -> 15.1 us  [exchange(): return lax.all_to_all(values, axes, 0, 0, tiled=True)]
where the time goes in v2:
time: 121 us; the launch traced here: 120 us
  blocking collectives  65.7 us (54%)
  Pallas kernels  20.5 us (17%)
  starting transfers between devices  16.8 us (14%)
  waiting for transfers between devices  15.1 us (12%)
  local copies, waits for them, and re-layouts  1.98 us (2%)
    all_to_all x4, blocking collectives, exchange(): return lax.all_to_all(values, axes, 0, 0, tiled=True)  65.7 us
    all_to_all x1, starting transfers between devices, exchange(): return lax.all_to_all(values, axes, 0, 0, tiled=True)  16.8 us
    all_to_all x1, waiting for transfers between devices, exchange(): return lax.all_to_all(values, axes, 0, 0, tiled=True)  15.1 us
    pallas_call x1, Pallas kernels, body(): call(fields_kernel, (shape(SUBS, 2 * N, 2 * N), shape(2 * N, N), jax.Shap...  7.46 us
    pallas_call x1, Pallas kernels, body(): call(products_kernel, shape(4 * N, N), smem(1) + vmem(4), 20, [pltpu.VMEM...  7.19 us
  transfers between devices with their start and end apart: 1, of which 1 were waited for; matrix products, arithmetic and copies ran while one was open for 0% of the time, Pallas kernels for 2%

profile of v2, /device:TPU:1, one launch (start us, length us, event | category | flops | bytes accessed | tf_op | source)
XLA Modules:
  0.0 120.3 jit_solution(3349875947511057240)
XLA Ops:
  0.0 0.0 copy-start.12
  0.0 0.0 copy-start.11
  0.0 0.0 copy-start.10
  0.0 0.0 copy-start.9
  0.0 0.0 copy-start.8
  0.0 0.0 copy-start.3
  0.0 0.0 copy-start.6
  0.0 2.4 %lines.1 = f32[1024,128]{1,0:T(8,128)} custom-call(f32[1,2,128,256]{3,2,1,0:T(8,128)} %orbital_ref.1, f32[1,2,128,256]{3,2,1,0:T(8,128)} %tangent_ref.3, s32[32,128]{1,0:T(8,128)} %bitcast.19, bf16[2,256,144]{2,1,0:T(8,128)(2,1)} %constant.30.clone.table_ref), custom_call_target="tpu_custom_call" | custom-call | tf_op jit(solution)/shard_map/lines/pallas_call | solution.py:601
  2.4 0.0 copy-start
  2.4 0.0 copy-start.2
  2.4 16.8 %all-to-all-start = ((f32[128,8,128]{2,1,0:T(8,128)}), f32[128,8,128]{2,1,0:T(8,128)S(1)}, u32[]{:S(2)}, u32[]{:S(2)}) async-start(f32[128,8,128]{2,1,0:T(8,128)} %bitcast.26), calls=%async_computation | async-start | bytes 1048576 | tf_op jit(solution)/shard_map/all_to_all | solution.py:581
  19.2 0.0 copy-done.12
  19.2 0.0 copy-done.11
  19.2 0.0 copy-done.10
  19.2 0.0 copy-done.9
  19.3 0.0 copy-done.8
  19.3 0.0 copy-done.3
  19.3 0.0 copy-start.4
  19.3 1.0 copy-done.4
  20.3 0.0 copy-start.7
  20.3 0.9 copy-done.7
  21.2 2.1 %ions.1.planes_ref = f32[3,128,128]{2,1,0:T(8,128)S(1)} custom-call(s32[8]{0:T(128)S(1)} %copy-done.11, s32[8]{0:T(128)S(1)} %copy-done.12, f32[3,2000]{1,0:T(4,128)S(1)} %bitcast.25, f32[2000]{0:T(1024)S(1)} %copy-done.9, f32[2000]{0:T(1024)S(1)} %copy-done.10, bf16[2,256,128]{2,1,0:T(8,128)(2,1)S(1)} %copy-done.7, f32[8,128,128]{2,1,0:T(8,128)S(1)} %copy-done.3, ...), custom_call_target="tpu_custom_call" | custom-call | tf_op jit(solution)/shard_map/ions/pallas_call | solution.py:603
  23.3 0.0 copy-done.6
  23.4 15.1 %all-to-all-done.lines_ref = f32[128,8,128]{2,1,0:T(8,128)S(1)} async-done(((f32[128,8,128]{2,1,0:T(8,128)}), f32[128,8,128]{2,1,0:T(8,128)S(1)}, u32[]{:S(2)}, u32[]{:S(2)}) %all-to-all-start) | async-done | bytes 524320 | tf_op jit(solution)/shard_map/all_to_all | solution.py:581
  38.5 0.0 copy-done
  38.5 0.0 copy-done.2
  38.5 7.5 %fields.1 = (f32[8,256,256]{2,1,0:T(8,128)S(1)}, f32[256,128]{1,0:T(8,128)S(1)}, bf16[2592,256]{1,0:T(8,128)(2,1)S(1)}) custom-call(s32[2048]{0:T(1024)S(1)} %bitcast.23, f32[128,8,128]{2,1,0:T(8,128)S(1)} %all-to-all-done.lines_ref, f32[3,128,128]{2,1,0:T(8,128)S(1)} %ions.1.planes_ref, bf16[1696,256]{1,0:T(8,128)(2,1)S(1)} %copy-done.2, ...), custom_call_target="tpu_custom_call" | custom-call | tf_op jit(solution)/shard_map/fields/pallas_call | solution.py:610
  45.9 19.3 %all_to_all.25 = f32[64,4,128]{2,1,0:T(4,128)S(1)} all-to-all(f32[64,4,128]{2,1,0:T(4,128)S(1)} %bitcast.21), channel_id=1, replica_groups=mesh['xl'=2,'yh'=4,'yl'=2,'core'=2,'xh'=2,'z'=8] {'xl','yh','yl','core',..., dimensions={0} | all-to-all | bytes 262144 | tf_op jit(solution)/shard_map/all_to_all | solution.py:581
  65.2 10.8 %all_to_all.26 = f32[8,32,128]{2,1,0:T(8,128)S(1)} all-to-all(f32[8,32,128]{2,1,0:T(8,128)S(1)} %bitcast.22), channel_id=1, replica_groups=mesh['xl'=2,'yh'=4,'yl'=2,'core'=2,'xh'=2,'z'=8] {'z'}, dimensions={0} | all-to-all | bytes 262144 | tf_op jit(solution)/shard_map/all_to_all | solution.py:581
  76.0 0.4 hartree.1
  76.5 17.2 %all_to_all.27 = f32[64,3,2,128]{3,2,1,0:T(2,128)S(1)} all-to-all(f32[64,3,2,128]{3,2,1,0:T(2,128)S(1)} %bitcast.16), channel_id=1, replica_groups=mesh['xl'=2,'yh'=4,'yl'=2,'core'=2,'xh'=2,'z'=8] {'xl','yh','yl','core',..., dimensions={0} | all-to-all | bytes 393216 | tf_op jit(solution)/shard_map/all_to_all | solution.py:581
  93.6 0.0 copy-start.1
  93.6 0.0 copy-start.5
  93.6 7.2 %products.1 = f32[512,128]{1,0:T(8,128)S(1)} custom-call(s32[2048]{0:T(1024)S(1)} %bitcast.24, f32[8,256,256]{2,1,0:T(8,128)S(1)} %get-tuple-element.10.fields_ref, f32[384,128]{1,0:T(8,128)S(1)} %bitcast.15, f32[3,128,128]{2,1,0:T(8,128)S(1)} %ions.1.planes_ref, bf16[2592,256]{1,0:T(8,128)(2,1)S(1)} %get-tuple-element.14.tables_ref), custom_call_target="tpu_custom_call" | custom-call | tf_op jit(solution)/shard_map/products/pallas_call | solution.py:627
  100.8 18.5 %all_to_all.28 = f32[128,4,128]{2,1,0:T(4,128)S(1)} all-to-all(f32[128,4,128]{2,1,0:T(4,128)S(1)} %bitcast.13), channel_id=1, replica_groups=mesh['xl'=2,'yh'=4,'yl'=2,'core'=2,'xh'=2,'z'=8] {'xl','yl','core','xh',..., dimensions={0} | all-to-all | bytes 524288 | tf_op jit(solution)/shard_map/all_to_all | solution.py:581
  119.3 0.0 copy-done.1
  119.3 0.0 copy-done.5
  119.3 0.9 result.1
  (3 shorter events, 0.0 us)
Async XLA Ops:
  0.0 19.2 %copy-start.12 = (s32[8]{0:T(128)S(1)}, s32[8]{0:T(128)}, u32[]{:S(2)}) copy-start(s32[8]{0:T(128)} %direction_ref.1) | copy-start | bytes 100
  0.0 19.2 %copy-start.11 = (s32[8]{0:T(128)S(1)}, s32[8]{0:T(128)}, u32[]{:S(2)}) copy-start(s32[8]{0:T(128)} %atom_ref.1) | copy-start | bytes 100
  0.0 19.2 %copy-start.10 = (f32[2000]{0:T(1024)S(1)}, f32[2000]{0:T(1024)}, u32[]{:S(2)}) copy-start(f32[2000]{0:T(1024)} %widths_ref.1) | copy-start | bytes 24004
  0.0 19.2 %copy-start.9 = (f32[2000]{0:T(1024)S(1)}, f32[2000]{0:T(1024)}, u32[]{:S(2)}) copy-start(f32[2000]{0:T(1024)} %charge_ref.1) | copy-start | bytes 24004
  0.0 19.2 %copy-start.8 = (f32[2000,3]{0,1:T(4,128)S(1)}, f32[2000,3]{0,1:T(4,128)}, u32[]{:S(2)}) copy-start(f32[2000,3]{0,1:T(4,128)} %param.20) | copy-start | bytes 72004
  0.0 19.2 %copy-start.3 = (f32[8,128,128]{2,1,0:T(8,128)S(1)}, f32[8,128,128]{2,1,0:T(8,128)}, u32[]{:S(2)}) copy-start(f32[8,128,128]{2,1,0:T(8,128)} %potential_ref.1) | copy-start | bytes 1572868
  0.0 23.3 %copy-start.6 = (s32[4096]{0:T(1024)S(1)}, s32[4096]{0:T(1024)}, u32[]{:S(2)}) copy-start(s32[4096]{0:T(1024)} %param.17) | copy-start | bytes 49156
  2.4 36.0 %copy-start = (bf16[2592,256]{1,0:T(8,128)(2,1)S(1)}, bf16[2592,256]{1,0:T(8,128)(2,1)}, u32[]{:S(2)}) copy-start(bf16[2592,256]{1,0:T(8,128)(2,1)} %constant.33.clone.late_ref) | copy-start | bytes 3981316
  2.4 36.0 %copy-start.2 = (bf16[1696,256]{1,0:T(8,128)(2,1)S(1)}, bf16[1696,256]{1,0:T(8,128)(2,1)}, u32[]{:S(2)}) copy-start(bf16[1696,256]{1,0:T(8,128)(2,1)} %constant.32.clone.tables) | copy-start | bytes 2605060
  2.4 36.0 %all-to-all-start = ((f32[128,8,128]{2,1,0:T(8,128)}), f32[128,8,128]{2,1,0:T(8,128)S(1)}, u32[]{:S(2)}, u32[]{:S(2)}) async-start(f32[128,8,128]{2,1,0:T(8,128)} %bitcast.26), calls=%async_computation | async-start | bytes 1048576 | tf_op jit(solution)/shard_map/all_to_all | solution.py:581
  19.3 1.0 copy-start.4
  20.3 0.9 copy-start.7
  93.6 25.7 %copy-start.1 = (f32[1,2,128,256]{3,2,1,0:T(8,128)S(1)}, f32[1,2,128,256]{3,2,1,0:T(8,128)}, u32[]{:S(2)}) copy-start(f32[1,2,128,256]{3,2,1,0:T(8,128)} %tangent_ref.3) | copy-start | bytes 786436
  93.6 25.7 %copy-start.5 = (bf16[2,144,256]{2,1,0:T(8,128)(2,1)S(1)}, bf16[2,144,256]{2,1,0:T(8,128)(2,1)}, u32[]{:S(2)}) copy-start(bf16[2,144,256]{2,1,0:T(8,128)(2,1)} %constant.34.clone.table_ref) | copy-start | bytes 442372

commit v3 on v2

--- a/solution.py
+++ b/solution.py
@@ -18,6 +18,8 @@
 LINE = 72
 SLABS = 68
 CELLS = SLABS * LINE
+PAIRS = 40
+TURNED_ROW = PAIRS + CUT
 DUMP = 65 * LINE
 CELL = 40.0
 SLATER = (3.0 / math.pi) ** (1.0 / 3.0)
@@ -91,28 +93,20 @@
 
 
 def x_forward_table():
-    frequency, kept = box_frequencies(LINE)
-    angle = angles(frequency, np.arange(N))
+    slot = np.concatenate([2 * np.arange(40), 2 * np.arange(40) + 1])
+    kept = (slot <= 2 * CUT).astype(np.float64)
+    angle = angles(slot - CUT, np.arange(N))
     cosine, sine = np.cos(angle) * kept[:, None], np.sin(angle) * kept[:, None]
-    return (np.block([[cosine, sine], [-sine, cosine]]))
+    real, imag = np.concatenate([cosine, sine], 1), np.concatenate([-sine, cosine], 1)
+    real[TURNED_ROW, :N] = 1.0
+    imag[TURNED_ROW, N:] = -1.0
+    return np.concatenate([real, imag])
 
 
 def y_forward_table():
-    frequency, kept = box_frequencies(N)
-    angle = angles(np.arange(N), frequency)
-    return (np.concatenate([np.cos(angle), np.sin(angle)], 1) * np.concatenate([kept, kept])[None, :])
-
-
-def spread_table():
-    table = np.zeros((N, 8, N))
-    for band in range(8):
-        for part in range(2):
-            for eighth in range(8):
-                for group in range(4):
-                    for half in range(2):
-                        table[band * 16 + part * 8 + eighth, eighth, band * 16 + group * 4 + part * 2 + half] = 1.0
-    table = table.reshape(N, 4, 2 * N).transpose(1, 0, 2)
-    return np.concatenate([table, table], 1).reshape(8 * N, 2 * N)
+    lane = np.arange(N) % 64
+    angle = angles(np.arange(N), np.where(lane <= CUT, lane, lane - 64))
+    return np.concatenate([np.cos(angle), np.sin(angle)], 1)
 
 
 def replicate_table():
@@ -184,8 +178,7 @@
             "real_turned": real_table().T,
             "x_forward": x_forward_table(),
             "y_forward": y_forward_table(),
-        },
-        {"spread": spread_table()},
+        }
 
     )
 
@@ -196,7 +189,8 @@
 
 def table_of(ref, places, name):
     high, low, rows, columns = places[name]
-    return ref[high : high + rows, 0:columns], ref[low : low + rows, 0:columns]
+    tall = low - high
+    return ref[high : high + tall, 0:columns][0:rows], ref[low : low + tall, 0:columns][0:rows]
 
 
 def early_table(ref, name):
@@ -268,11 +262,8 @@
 
 
 def fields_kernel(
-    dest_ref, lines_ref, planes_ref, tables, late_ref, fields_ref, sums_ref, late_out, turned, grid, middle, arrival
+    dest_ref, lines_ref, tables, fields_ref, sums_ref, turned, grid, middle
 ):
-    del planes_ref
-    copy = pltpu.make_async_copy(late_ref, late_out, arrival)
-    copy.start()
     replicate = tables[EARLY_PLACES["replicate"] : EARLY_PLACES["replicate"] + 4 * N, :]
     lower = lax.broadcasted_iota(jnp.int32, (8, N), 0) < 4
     for quad in range(4):
@@ -348,7 +339,6 @@
     for half in range(2):
         sums_ref[pl.ds(half, 64, stride=4), :] = density[half * 64 : half * 64 + 64]
         sums_ref[pl.ds(2 + half, 64, stride=4), :] = spectrum[half * 64 : half * 64 + 64]
-    copy.wait()
 
 
 def mix_kernel(arrived_ref, sums_ref, spread_ref):
@@ -412,17 +402,25 @@
     table_ref,
     potential_ref,
     core_ref,
+    early_ref,
+    late_ref,
+    lines_ref,
     out_ref,
+    early_out,
+    late_out,
     centres,
     spreads,
     marks,
     charges,
     arrivals,
 ):
+    del lines_ref
     own = lax.axis_index(("xl", "yl", "core"))
     copies = [
         pltpu.make_async_copy(potential_ref.at[own], out_ref.at[0], arrivals.at[0]),
         pltpu.make_async_copy(core_ref.at[own], out_ref.at[1], arrivals.at[1]),
+        pltpu.make_async_copy(early_ref, early_out, arrivals.at[2]),
+        pltpu.make_async_copy(late_ref, late_out, arrivals.at[3]),
     ]
     for copy in copies:
         copy.start()
@@ -455,17 +453,7 @@
         copy.wait()
 
 
-def products_kernel(
-    dest_ref,
-    fields_ref,
-    solved_ref,
-    planes_ref,
-    tables_ref,
-    out_ref,
-    lines,
-    grid,
-    gathered,
-):
+def products_kernel(columns_ref, fields_ref, solved_ref, planes_ref, tables_ref, out_ref, lines):
     def solved(which):
         return jnp.concatenate([solved_ref[pl.ds(which * 2 + half, 64, stride=6), :] for half in range(2)], 0)
 
@@ -481,7 +469,7 @@
     ytable = late_table(tables_ref, "y_forward")
     effective2 = jnp.concatenate([effective, effective], 0)
     change2 = jnp.concatenate([change, change], 0)
-    blocks = [[], []]
+    lower = lax.broadcasted_iota(jnp.int32, (PAIRS, N), 1) < 64
     for couple in range(SUBS // 2):
         sides = []
         for band in (2 * couple, 2 * couple + 1):
@@ -490,45 +478,32 @@
         rows = jnp.concatenate([across[:, 0:N], across[:, N : 2 * N]], 0)
         done = dot3(halves(rows), ytable)
         for side in range(2):
-            real = done[side * 144 : side * 144 + 72]
-            imag = done[side * 144 + 72 : side * 144 + 144]
-            base = (2 * couple + side) * 144
-            lines[base : base + 72, :] = real[:, 0:N] + imag[:, N : 2 * N]
-            lines[base + 72 : base + 144, :] = imag[:, 0:N] - real[:, N : 2 * N]
-    first = LATE_PLACES["spread"]
-    spread = [tables_ref[first + block * 2 * N : first + (block + 1) * 2 * N, :] for block in range(4)]
-    for eight in range(9):
-        tiles = [lines[half * 72 + eight * 8 : half * 72 + eight * 8 + 8, :] for half in range(16)]
-        turned = jnp.concatenate(tiles, 0).T[0:LINE]
-        high, low = halves(turned)
-        both = jnp.concatenate([high, low], 1)
-        for block in range(4):
-            cells = dot(both, spread[block])
-            for side in range(2):
-                base = (eight * 8 + block * 2 + side) * LINE
-                grid[base : base + LINE, :] = cells[:, side * N : (side + 1) * N]
-    lane = lax.broadcasted_iota(jnp.int32, (1, N), 1)
-    slot_of_lane = ((lane // 4) % 4) * 2 + lane % 2
-    masks = [slot_of_lane == slot for slot in range(1, 8)]
-    for block in range(4):
-
-        def gather(step, carry, block=block):
-            for inner in range(8):
-                stick = step * 8 + inner
-                row = None
-                for slot in range(4):
-                    places = dest_ref[(4 * block + slot) * N + stick]
-                    cells = [grid[pl.ds(places & 0xFFFF, 1), :], grid[pl.ds(places >> 16, 1), :]]
-                    for half in range(2):
-                        row = cells[half] if row is None else jnp.where(masks[2 * slot + half - 1], cells[half], row)
-                gathered[pl.ds(stick, 1), :] = row
-            return carry
-
-        lax.fori_loop(0, N // 8, gather, 0)
-        turned = gathered[...].T
-        for band in range(SUBS):
-            base = band * 64 + block * 16
-            out_ref[base : base + 16, :] = turned[band * 16 : band * 16 + 16]
+            real = done[side * 4 * PAIRS : side * 4 * PAIRS + 2 * PAIRS]
+            imag = done[side * 4 * PAIRS + 2 * PAIRS : (side + 1) * 4 * PAIRS]
+            whole = (real[:, 0:N] + imag[:, N : 2 * N], imag[:, 0:N] - real[:, N : 2 * N])
+            for part in range(2):
+                base = (part * SUBS + 2 * couple + side) * PAIRS
+                lines[base : base + PAIRS, :] = jnp.where(lower, whole[part][0:PAIRS], whole[part][PAIRS : 2 * PAIRS])
+    across, inplane = stick_frequencies(columns_ref[...])
+    box = across + CUT
+    special = jnp.logical_and(across == 0, inplane == -CUT)
+    place = jnp.where(special, 64 + CUT, (box & 1) * 64 + (inplane & 63))
+    held = jnp.where(special, CUT, box >> 1)
+    held = jnp.where(across * across + inplane * inplane <= CUT * CUT, held, -1)
+    sign = jnp.where(special, -1.0, 1.0)
+    for vector in range(2 * GROUPS):
+        index = jnp.broadcast_to(place[vector : vector + 1], (SUBS, N))
+        wanted = jnp.broadcast_to(held[vector : vector + 1], (SUBS, N))
+        picked = [jnp.zeros((SUBS, N), f32)] * 2
+        for couple in range(CUT + 1):
+            mask = wanted == couple
+            for part in range(2):
+                cells = lines[pl.ds(part * SUBS * PAIRS + couple, SUBS, stride=PAIRS), :]
+                picked[part] = jnp.where(mask, jnp.take_along_axis(cells, index, axis=1), picked[part])
+        picked[1] = picked[1] * sign[vector : vector + 1]
+        for part in range(2):
+            row = (vector // 2) * 4 + part * 2 + vector % 2
+            out_ref[pl.ds(row, SUBS, stride=64), :] = picked[part]
 
 
 def result_kernel(arrived_ref, tangent_ref, columns_ref, table_ref, out_ref):
@@ -575,6 +550,10 @@
         compiler_params=pltpu.CompilerParams(vmem_limit_bytes=(mebibytes << 20) or None),
         name=kernel.__name__.removesuffix("_kernel"),
     )
+
+
+def stay(values):
+    return pltpu.with_memory_space_constraint(jnp.asarray(values), pltpu.HBM)
 
 
 def exchange(values, axes):
@@ -598,48 +577,47 @@
     cell = (across + CUT) * LINE + (inplane + CUT)
     dest = jnp.where(across * across + inplane * inplane <= CUT * CUT, cell, DUMP).reshape(GROUPS, 2, N)
     dest = (dest[:, 0] + dest[:, 1] * 65536).reshape(-1)
-    lines = call(lines_kernel, shape(N * 8, N), vmem(4), 0)(orbitals, orbital_tangent, columns, z_inverse_table())
-    lines = exchange(lines.reshape(N, 8, N), PLANE_AXES)
-    planes = call(
+    lines = call(lines_kernel, pltpu.VMEM((N * 8, N), f32), vmem(4), 8)(
+        stay(orbitals), stay(orbital_tangent), stay(columns), stay(z_inverse_table())
+    )
+    arrived = exchange(lines.reshape(N, 8, N), PLANE_AXES)
+    planes, early, late = call(
         ions_kernel,
-        shape(3, N, N),
-        smem(5) + vmem(1) + anywhere(2),
-        4,
-        [pltpu.VMEM((24, N), f32)] * 3 + [pltpu.VMEM((8, N), f32), pltpu.SemaphoreType.DMA((2,))],
-    )(atom_index, direction, positions.T, z_charge, widths, profile_table(), ion_potential, core_density)
-    fields, sums, tables = call(
+        (pltpu.VMEM((3, N, N), f32), pltpu.VMEM(EARLY.shape, bf16), pltpu.VMEM(LATE.shape, bf16)),
+        smem(5) + vmem(1) + anywhere(5),
+        8,
+        [pltpu.VMEM((24, N), f32)] * 3 + [pltpu.VMEM((8, N), f32), pltpu.SemaphoreType.DMA((4,))],
+    )(
+        atom_index,
+        direction,
+        positions.T,
+        z_charge,
+        widths,
+        profile_table(),
+        stay(ion_potential),
+        stay(core_density),
+        stay(EARLY),
+        stay(LATE),
+        lines,
+    )
+    fields, sums = call(
         fields_kernel,
-        (shape(SUBS, 2 * N, 2 * N), shape(2 * N, N), jax.ShapeDtypeStruct(LATE.shape, bf16)),
-        smem(1) + vmem(1) + anywhere(1) + vmem(1) + anywhere(1),
-        24,
+        (shape(SUBS, 2 * N, 2 * N), shape(2 * N, N)),
+        smem(1) + vmem(2),
+        20,
         [
             pltpu.VMEM((4, 8 * N, N), f32),
             pltpu.VMEM((CELLS, N), f32),
             pltpu.VMEM((24 * PITCH, N), f32),
-            pltpu.SemaphoreType.DMA,
         ],
-    )(dest, lines, planes, EARLY, LATE)
+    )(dest, arrived, early)
     sums = exchange(sums.reshape(64, 4, N), BAND_AXES + ("xh",)).reshape(2 * N, N)
     sums, spectrum = call(mix_kernel, (shape(64, N), shape(2 * N, N)), vmem(1), 4)(sums)
     spectrum = exchange(spectrum.reshape(8, 32, N), "z").reshape(2 * N, N)
-    solved = call(hartree_kernel, shape(3 * N, N), vmem(3), 4)(sums, spectrum, tables)
+    solved = call(hartree_kernel, shape(3 * N, N), vmem(3), 4)(sums, spectrum, late)
     solved = exchange(solved.reshape(64, 3, 2, N), BAND_AXES + ("xh",)).reshape(3 * N, N)
-    outgoing = call(
-        products_kernel,
-        shape(4 * N, N),
-        smem(1) + vmem(4),
-        20,
-        [
-            pltpu.VMEM((16 * LINE, N), f32),
-            pltpu.VMEM((LINE * LINE, N), f32),
-            pltpu.VMEM((N, N), f32),
-        ],
-    )(
-        dest,
-        fields,
-        solved,
-        planes,
-        tables,
+    outgoing = call(products_kernel, shape(4 * N, N), vmem(5), 20, [pltpu.VMEM((16 * PAIRS, N), f32)])(
+        columns, fields, solved, planes, late
     )
     arrived = exchange(outgoing.reshape(N, 4, N), PLANE_AXES).reshape(4 * N, N)
     return call(result_kernel, shape(1, 2, N, 256), vmem(4), 8)(arrived, orbital_tangent, columns, z_forward_table())

time: 121 us -> 118 us (0.975)
  local copies, waits for them, and re-layouts: 1.98 us -> 0.03 us
  Pallas kernels: 20.5 us -> 18.6 us
    unnamed x26 -> x18, local copies, waits for them, and re-layouts: 1.98 us -> 0.03 us
    pallas_call x5, Pallas kernels: 19.6 us -> 17.6 us  [the longest x1 7.28 us: body(): call(fields_kernel, (shape(SUBS, 2 * N, 2 * N), shape(2 * N, N)), smem(1)...]
  transfers between devices with their start and end apart: 1 -> 1, of which waited for: 1 -> 1; matrix products, arithmetic and copies ran while one was open for 0% -> 0% of each run, Pallas kernels for 2% -> 3%
where the time goes in v3:
time: 118 us; the launch traced here: 117 us
  blocking collectives  65.7 us (56%)
  Pallas kernels  18.6 us (16%)
  starting transfers between devices  16.8 us (14%)
  waiting for transfers between devices  16.1 us (14%)
    all_to_all x4, blocking collectives, exchange(): return lax.all_to_all(values, axes, 0, 0, tiled=True)  65.7 us
    all_to_all x1, starting transfers between devices, exchange(): return lax.all_to_all(values, axes, 0, 0, tiled=True)  16.8 us
    all_to_all x1, waiting for transfers between devices, exchange(): return lax.all_to_all(values, axes, 0, 0, tiled=True)  16.1 us
    pallas_call x1, Pallas kernels, body(): call(fields_kernel, (shape(SUBS, 2 * N, 2 * N), shape(2 * N, N)), smem(1)...  7.28 us
    pallas_call x1, Pallas kernels, body(): call(products_kernel, shape(4 * N, N), vmem(5), 20, [pltpu.VMEM((16 * PAI...  4.47 us
    pallas_call x1, Pallas kernels, body(): call(ions_kernel, (pltpu.VMEM((3, N, N), f32), pltpu.VMEM(EARLY.shape, bf...  3.03 us
    pallas_call x1, Pallas kernels, body(): call(lines_kernel, pltpu.VMEM((N * 8, N), f32), vmem(4), 8)  2.41 us
  transfers between devices with their start and end apart: 1, of which 1 were waited for; matrix products, arithmetic and copies ran while one was open for 0% of the time, Pallas kernels for 3%

profile of v3, /device:TPU:1, one launch (start us, length us, event | category | flops | bytes accessed | tf_op | source)
XLA Modules:
  0.0 117.4 jit_solution(12195276564667117644)
XLA Ops:
  0.0 0.0 copy-start.3
  0.0 0.0 copy-start.8
  0.0 0.0 copy-start.7
  0.0 0.0 copy-start.6
  0.0 0.0 copy-start.5
  0.0 0.0 copy-start.4
  0.0 2.4 %lines.1.lines_ref = f32[1024,128]{1,0:T(8,128)} custom-call(f32[1,2,128,256]{3,2,1,0:T(8,128)} %orbital_ref.1, f32[1,2,128,256]{3,2,1,0:T(8,128)} %tangent_ref.3, s32[32,128]{1,0:T(8,128)} %bitcast.19, bf16[2,256,144]{2,1,0:T(8,128)(2,1)} %constant.30.clone.table_ref), custom_call_target="tpu_custom_call" | custom-call | tf_op jit(solution)/shard_map/lines/pallas_call | solution.py:580
  2.5 0.0 copy-start.1
  2.5 16.8 %all-to-all-start = ((f32[128,8,128]{2,1,0:T(8,128)}), f32[128,8,128]{2,1,0:T(8,128)S(1)}, u32[]{:S(2)}, u32[]{:S(2)}) async-start(f32[128,8,128]{2,1,0:T(8,128)} %bitcast.3), calls=%async_computation | async-start | bytes 1048576 | tf_op jit(solution)/shard_map/all_to_all | solution.py:560
  19.2 0.0 copy-done.3
  19.2 0.0 copy-done.8
  19.3 0.0 copy-done.7
  19.3 0.0 copy-done.6
  19.3 0.0 copy-done.5
  19.3 0.0 copy-done.4
  19.3 3.0 %ions.1 = (f32[3,128,128]{2,1,0:T(8,128)S(1)}, bf16[1696,256]{1,0:T(8,128)(2,1)S(1)}, bf16[1600,256]{1,0:T(8,128)(2,1)S(1)}) custom-call(s32[8]{0:T(128)S(1)} %copy-done.7, s32[8]{0:T(128)S(1)} %copy-done.8, f32[3,2000]{1,0:T(4,128)S(1)} %bitcast.24, f32[2000]{0:T(1024)S(1)} %copy-done.5, f32[2000]{0:T(1024)S(1)} %copy-done.6, ...), custom_call_target="tpu_custom_call" | custom-call | tf_op jit(solution)/shard_map/ions/pallas_call | solution.py:584
  22.3 0.0 copy-done.1
  22.4 16.1 %all-to-all-done.lines_ref = f32[128,8,128]{2,1,0:T(8,128)S(1)} async-done(((f32[128,8,128]{2,1,0:T(8,128)}), f32[128,8,128]{2,1,0:T(8,128)S(1)}, u32[]{:S(2)}, u32[]{:S(2)}) %all-to-all-start) | async-done | bytes 524320 | tf_op jit(solution)/shard_map/all_to_all | solution.py:560
  38.5 7.3 %fields.1 = (f32[8,256,256]{2,1,0:T(8,128)S(1)}, f32[256,128]{1,0:T(8,128)S(1)}) custom-call(s32[2048]{0:T(1024)S(1)} %bitcast.25, f32[128,8,128]{2,1,0:T(8,128)S(1)} %all-to-all-done.lines_ref, bf16[1696,256]{1,0:T(8,128)(2,1)S(1)} %get-tuple-element.12.tables), custom_call_target="tpu_custom_call" | custom-call | tf_op jit(solution)/shard_map/fields/pallas_call | solution.py:603
  45.8 19.3 %all_to_all.25 = f32[64,4,128]{2,1,0:T(4,128)S(1)} all-to-all(f32[64,4,128]{2,1,0:T(4,128)S(1)} %bitcast.22), channel_id=1, replica_groups=mesh['xl'=2,'yh'=4,'yl'=2,'core'=2,'xh'=2,'z'=8] {'xl','yh','yl','core',..., dimensions={0} | all-to-all | bytes 262144 | tf_op jit(solution)/shard_map/all_to_all | solution.py:560
  65.1 10.8 %all_to_all.26 = f32[8,32,128]{2,1,0:T(8,128)S(1)} all-to-all(f32[8,32,128]{2,1,0:T(8,128)S(1)} %bitcast.23), channel_id=1, replica_groups=mesh['xl'=2,'yh'=4,'yl'=2,'core'=2,'xh'=2,'z'=8] {'z'}, dimensions={0} | all-to-all | bytes 262144 | tf_op jit(solution)/shard_map/all_to_all | solution.py:560
  75.8 0.4 hartree.1
  76.3 17.2 %all_to_all.27 = f32[64,3,2,128]{3,2,1,0:T(2,128)S(1)} all-to-all(f32[64,3,2,128]{3,2,1,0:T(2,128)S(1)} %bitcast.16), channel_id=1, replica_groups=mesh['xl'=2,'yh'=4,'yl'=2,'core'=2,'xh'=2,'z'=8] {'xl','yh','yl','core',..., dimensions={0} | all-to-all | bytes 393216 | tf_op jit(solution)/shard_map/all_to_all | solution.py:560
  93.5 0.0 copy-start
  93.5 0.0 copy-start.2
  93.5 4.5 %products.1 = f32[512,128]{1,0:T(8,128)S(1)} custom-call(s32[32,128]{1,0:T(8,128)S(1)} %bitcast.20, f32[8,256,256]{2,1,0:T(8,128)S(1)} %get-tuple-element.13.fields_ref, f32[384,128]{1,0:T(8,128)S(1)} %bitcast.15, f32[3,128,128]{2,1,0:T(8,128)S(1)} %get-tuple-element.18.planes_ref, bf16[1600,256]{1,0:T(8,128)(2,1)S(1)} %get-tuple-element.17.tables_ref), custom_call_target="tpu_custom_call" | custom-call | tf_op jit(solution)/shard_map/products/pallas_call | solution.py:619
  97.9 18.5 %all_to_all.28 = f32[128,4,128]{2,1,0:T(4,128)S(1)} all-to-all(f32[128,4,128]{2,1,0:T(4,128)S(1)} %bitcast.13), channel_id=1, replica_groups=mesh['xl'=2,'yh'=4,'yl'=2,'core'=2,'xh'=2,'z'=8] {'xl','yl','core','xh',..., dimensions={0} | all-to-all | bytes 524288 | tf_op jit(solution)/shard_map/all_to_all | solution.py:560
  116.5 0.0 copy-done
  116.5 0.0 copy-done.2
  116.5 0.9 result.1
  (3 shorter events, 0.0 us)
Async XLA Ops:
  0.0 19.2 %copy-start.3 = (bf16[2,256,128]{2,1,0:T(8,128)(2,1)S(1)}, bf16[2,256,128]{2,1,0:T(8,128)(2,1)}, u32[]{:S(2)}) copy-start(bf16[2,256,128]{2,1,0:T(8,128)(2,1)} %constant.33.clone.table_ref) | copy-start | bytes 393220
  0.0 19.2 %copy-start.8 = (s32[8]{0:T(128)S(1)}, s32[8]{0:T(128)}, u32[]{:S(2)}) copy-start(s32[8]{0:T(128)} %direction_ref.1) | copy-start | bytes 100
  0.0 19.2 %copy-start.7 = (s32[8]{0:T(128)S(1)}, s32[8]{0:T(128)}, u32[]{:S(2)}) copy-start(s32[8]{0:T(128)} %atom_ref.1) | copy-start | bytes 100
  0.0 19.3 %copy-start.6 = (f32[2000]{0:T(1024)S(1)}, f32[2000]{0:T(1024)}, u32[]{:S(2)}) copy-start(f32[2000]{0:T(1024)} %widths_ref.1) | copy-start | bytes 24004
  0.0 19.3 %copy-start.5 = (f32[2000]{0:T(1024)S(1)}, f32[2000]{0:T(1024)}, u32[]{:S(2)}) copy-start(f32[2000]{0:T(1024)} %charge_ref.1) | copy-start | bytes 24004
  0.0 19.3 %copy-start.4 = (f32[2000,3]{0,1:T(4,128)S(1)}, f32[2000,3]{0,1:T(4,128)}, u32[]{:S(2)}) copy-start(f32[2000,3]{0,1:T(4,128)} %param.20) | copy-start | bytes 72004
  2.5 19.9 %copy-start.1 = (s32[4096]{0:T(1024)S(1)}, s32[4096]{0:T(1024)}, u32[]{:S(2)}) copy-start(s32[4096]{0:T(1024)} %param.17) | copy-start | bytes 49156
  2.5 36.0 %all-to-all-start = ((f32[128,8,128]{2,1,0:T(8,128)}), f32[128,8,128]{2,1,0:T(8,128)S(1)}, u32[]{:S(2)}, u32[]{:S(2)}) async-start(f32[128,8,128]{2,1,0:T(8,128)} %bitcast.3), calls=%async_computation | async-start | bytes 1048576 | tf_op jit(solution)/shard_map/all_to_all | solution.py:560
  93.5 23.0 %copy-start = (f32[1,2,128,256]{3,2,1,0:T(8,128)S(1)}, f32[1,2,128,256]{3,2,1,0:T(8,128)}, u32[]{:S(2)}) copy-start(f32[1,2,128,256]{3,2,1,0:T(8,128)} %tangent_ref.3) | copy-start | bytes 786436
  93.5 23.0 %copy-start.2 = (bf16[2,144,256]{2,1,0:T(8,128)(2,1)S(1)}, bf16[2,144,256]{2,1,0:T(8,128)(2,1)}, u32[]{:S(2)}) copy-start(bf16[2,144,256]{2,1,0:T(8,128)(2,1)} %constant.34.clone.table_ref) | copy-start | bytes 442372

commit v4 on v3

--- a/solution.py
+++ b/solution.py
@@ -453,7 +453,7 @@
         copy.wait()
 
 
-def products_kernel(columns_ref, fields_ref, solved_ref, planes_ref, tables_ref, out_ref, lines):
+def products_kernel(columns_ref, fields_ref, solved_ref, planes_ref, tables_ref, out_ref, lines, cells):
     def solved(which):
         return jnp.concatenate([solved_ref[pl.ds(which * 2 + half, 64, stride=6), :] for half in range(2)], 0)
 
@@ -484,6 +484,10 @@
             for part in range(2):
                 base = (part * SUBS + 2 * couple + side) * PAIRS
                 lines[base : base + PAIRS, :] = jnp.where(lower, whole[part][0:PAIRS], whole[part][PAIRS : 2 * PAIRS])
+    for couple in range(CUT + 1):
+        for part in range(2):
+            at = (couple * 2 + part) * SUBS
+            cells[at : at + SUBS, :] = lines[pl.ds(part * SUBS * PAIRS + couple, SUBS, stride=PAIRS), :]
     across, inplane = stick_frequencies(columns_ref[...])
     box = across + CUT
     special = jnp.logical_and(across == 0, inplane == -CUT)
@@ -498,8 +502,9 @@
         for couple in range(CUT + 1):
             mask = wanted == couple
             for part in range(2):
-                cells = lines[pl.ds(part * SUBS * PAIRS + couple, SUBS, stride=PAIRS), :]
-                picked[part] = jnp.where(mask, jnp.take_along_axis(cells, index, axis=1), picked[part])
+                at = (couple * 2 + part) * SUBS
+                found = jnp.take_along_axis(cells[at : at + SUBS, :], index, axis=1)
+                picked[part] = jnp.where(mask, found, picked[part])
         picked[1] = picked[1] * sign[vector : vector + 1]
         for part in range(2):
             row = (vector // 2) * 4 + part * 2 + vector % 2
@@ -616,7 +621,7 @@
     spectrum = exchange(spectrum.reshape(8, 32, N), "z").reshape(2 * N, N)
     solved = call(hartree_kernel, shape(3 * N, N), vmem(3), 4)(sums, spectrum, late)
     solved = exchange(solved.reshape(64, 3, 2, N), BAND_AXES + ("xh",)).reshape(3 * N, N)
-    outgoing = call(products_kernel, shape(4 * N, N), vmem(5), 20, [pltpu.VMEM((16 * PAIRS, N), f32)])(
+    outgoing = call(products_kernel, shape(4 * N, N), vmem(5), 20, [pltpu.VMEM((16 * PAIRS, N), f32), pltpu.VMEM((66 * SUBS, N), f32)])(
         columns, fields, solved, planes, late
     )
     arrived = exchange(outgoing.reshape(N, 4, N), PLANE_AXES).reshape(4 * N, N)

time: 118 us -> 118 us (level)
  no operation moved by 1% of the time
where the time goes in v4:
time: 118 us; the launch traced here: 117 us
  blocking collectives  65.7 us (56%)
  Pallas kernels  18.6 us (16%)
  starting transfers between devices  16.8 us (14%)
  waiting for transfers between devices  16.1 us (14%)
    all_to_all x4, blocking collectives, exchange(): return lax.all_to_all(values, axes, 0, 0, tiled=True)  65.7 us
    all_to_all x1, starting transfers between devices, exchange(): return lax.all_to_all(values, axes, 0, 0, tiled=True)  16.8 us
    all_to_all x1, waiting for transfers between devices, exchange(): return lax.all_to_all(values, axes, 0, 0, tiled=True)  16.1 us
    pallas_call x1, Pallas kernels, body(): call(fields_kernel, (shape(SUBS, 2 * N, 2 * N), shape(2 * N, N)), smem(1)...  7.28 us
    pallas_call x1, Pallas kernels, body(): call(products_kernel, shape(4 * N, N), vmem(5), 20, [pltpu.VMEM((16 * PAI...  4.43 us
    pallas_call x1, Pallas kernels, body(): call(ions_kernel, (pltpu.VMEM((3, N, N), f32), pltpu.VMEM(EARLY.shape, bf...  3.03 us
    pallas_call x1, Pallas kernels, body(): call(lines_kernel, pltpu.VMEM((N * 8, N), f32), vmem(4), 8)  2.41 us
  transfers between devices with their start and end apart: 1, of which 1 were waited for; matrix products, arithmetic and copies ran while one was open for 0% of the time, Pallas kernels for 3%

profile of v4, /device:TPU:1, one launch (start us, length us, event | category | flops | bytes accessed | tf_op | source)
XLA Modules:
  0.0 117.4 jit_solution(957471562223537162)
XLA Ops:
  0.0 0.0 copy-start.3
  0.0 0.0 copy-start.8
  0.0 0.0 copy-start.7
  0.0 0.0 copy-start.6
  0.0 0.0 copy-start.5
  0.0 0.0 copy-start.4
  0.0 2.4 %lines.1.lines_ref = f32[1024,128]{1,0:T(8,128)} custom-call(f32[1,2,128,256]{3,2,1,0:T(8,128)} %orbital_ref.1, f32[1,2,128,256]{3,2,1,0:T(8,128)} %tangent_ref.3, s32[32,128]{1,0:T(8,128)} %bitcast.19, bf16[2,256,144]{2,1,0:T(8,128)(2,1)} %constant.30.clone.table_ref), custom_call_target="tpu_custom_call" | custom-call | tf_op jit(solution)/shard_map/lines/pallas_call | solution.py:585
  2.5 0.0 copy-start.1
  2.5 16.8 %all-to-all-start = ((f32[128,8,128]{2,1,0:T(8,128)}), f32[128,8,128]{2,1,0:T(8,128)S(1)}, u32[]{:S(2)}, u32[]{:S(2)}) async-start(f32[128,8,128]{2,1,0:T(8,128)} %bitcast.3), calls=%async_computation | async-start | bytes 1048576 | tf_op jit(solution)/shard_map/all_to_all | solution.py:565
  19.2 0.0 copy-done.3
  19.2 0.0 copy-done.8
  19.3 0.0 copy-done.7
  19.3 0.0 copy-done.6
  19.3 0.0 copy-done.5
  19.3 0.0 copy-done.4
  19.3 3.0 %ions.1 = (f32[3,128,128]{2,1,0:T(8,128)S(1)}, bf16[1696,256]{1,0:T(8,128)(2,1)S(1)}, bf16[1600,256]{1,0:T(8,128)(2,1)S(1)}) custom-call(s32[8]{0:T(128)S(1)} %copy-done.7, s32[8]{0:T(128)S(1)} %copy-done.8, f32[3,2000]{1,0:T(4,128)S(1)} %bitcast.24, f32[2000]{0:T(1024)S(1)} %copy-done.5, f32[2000]{0:T(1024)S(1)} %copy-done.6, ...), custom_call_target="tpu_custom_call" | custom-call | tf_op jit(solution)/shard_map/ions/pallas_call | solution.py:589
  22.3 0.0 copy-done.1
  22.4 16.1 %all-to-all-done.lines_ref = f32[128,8,128]{2,1,0:T(8,128)S(1)} async-done(((f32[128,8,128]{2,1,0:T(8,128)}), f32[128,8,128]{2,1,0:T(8,128)S(1)}, u32[]{:S(2)}, u32[]{:S(2)}) %all-to-all-start) | async-done | bytes 524320 | tf_op jit(solution)/shard_map/all_to_all | solution.py:565
  38.5 7.3 %fields.1 = (f32[8,256,256]{2,1,0:T(8,128)S(1)}, f32[256,128]{1,0:T(8,128)S(1)}) custom-call(s32[2048]{0:T(1024)S(1)} %bitcast.25, f32[128,8,128]{2,1,0:T(8,128)S(1)} %all-to-all-done.lines_ref, bf16[1696,256]{1,0:T(8,128)(2,1)S(1)} %get-tuple-element.12.tables), custom_call_target="tpu_custom_call" | custom-call | tf_op jit(solution)/shard_map/fields/pallas_call | solution.py:608
  45.8 19.3 %all_to_all.25 = f32[64,4,128]{2,1,0:T(4,128)S(1)} all-to-all(f32[64,4,128]{2,1,0:T(4,128)S(1)} %bitcast.22), channel_id=1, replica_groups=mesh['xl'=2,'yh'=4,'yl'=2,'core'=2,'xh'=2,'z'=8] {'xl','yh','yl','core',..., dimensions={0} | all-to-all | bytes 262144 | tf_op jit(solution)/shard_map/all_to_all | solution.py:565
  65.1 10.8 %all_to_all.26 = f32[8,32,128]{2,1,0:T(8,128)S(1)} all-to-all(f32[8,32,128]{2,1,0:T(8,128)S(1)} %bitcast.23), channel_id=1, replica_groups=mesh['xl'=2,'yh'=4,'yl'=2,'core'=2,'xh'=2,'z'=8] {'z'}, dimensions={0} | all-to-all | bytes 262144 | tf_op jit(solution)/shard_map/all_to_all | solution.py:565
  75.8 0.4 hartree.1
  76.3 17.2 %all_to_all.27 = f32[64,3,2,128]{3,2,1,0:T(2,128)S(1)} all-to-all(f32[64,3,2,128]{3,2,1,0:T(2,128)S(1)} %bitcast.16), channel_id=1, replica_groups=mesh['xl'=2,'yh'=4,'yl'=2,'core'=2,'xh'=2,'z'=8] {'xl','yh','yl','core',..., dimensions={0} | all-to-all | bytes 393216 | tf_op jit(solution)/shard_map/all_to_all | solution.py:565
  93.5 0.0 copy-start
  93.5 0.0 copy-start.2
  93.5 4.4 %products.1 = f32[512,128]{1,0:T(8,128)S(1)} custom-call(s32[32,128]{1,0:T(8,128)S(1)} %bitcast.20, f32[8,256,256]{2,1,0:T(8,128)S(1)} %get-tuple-element.13.fields_ref, f32[384,128]{1,0:T(8,128)S(1)} %bitcast.15, f32[3,128,128]{2,1,0:T(8,128)S(1)} %get-tuple-element.18.planes_ref, bf16[1600,256]{1,0:T(8,128)(2,1)S(1)} %get-tuple-element.17.tables_ref), custom_call_target="tpu_custom_call" | custom-call | tf_op jit(solution)/shard_map/products/pallas_call | solution.py:624
  97.9 18.5 %all_to_all.28 = f32[128,4,128]{2,1,0:T(4,128)S(1)} all-to-all(f32[128,4,128]{2,1,0:T(4,128)S(1)} %bitcast.13), channel_id=1, replica_groups=mesh['xl'=2,'yh'=4,'yl'=2,'core'=2,'xh'=2,'z'=8] {'xl','yl','core','xh',..., dimensions={0} | all-to-all | bytes 524288 | tf_op jit(solution)/shard_map/all_to_all | solution.py:565
  116.4 0.0 copy-done
  116.4 0.0 copy-done.2
  116.4 0.9 result.1
  (3 shorter events, 0.0 us)
Async XLA Ops:
  0.0 19.2 %copy-start.3 = (bf16[2,256,128]{2,1,0:T(8,128)(2,1)S(1)}, bf16[2,256,128]{2,1,0:T(8,128)(2,1)}, u32[]{:S(2)}) copy-start(bf16[2,256,128]{2,1,0:T(8,128)(2,1)} %constant.33.clone.table_ref) | copy-start | bytes 393220
  0.0 19.2 %copy-start.8 = (s32[8]{0:T(128)S(1)}, s32[8]{0:T(128)}, u32[]{:S(2)}) copy-start(s32[8]{0:T(128)} %direction_ref.1) | copy-start | bytes 100
  0.0 19.2 %copy-start.7 = (s32[8]{0:T(128)S(1)}, s32[8]{0:T(128)}, u32[]{:S(2)}) copy-start(s32[8]{0:T(128)} %atom_ref.1) | copy-start | bytes 100
  0.0 19.3 %copy-start.6 = (f32[2000]{0:T(1024)S(1)}, f32[2000]{0:T(1024)}, u32[]{:S(2)}) copy-start(f32[2000]{0:T(1024)} %widths_ref.1) | copy-start | bytes 24004
  0.0 19.3 %copy-start.5 = (f32[2000]{0:T(1024)S(1)}, f32[2000]{0:T(1024)}, u32[]{:S(2)}) copy-start(f32[2000]{0:T(1024)} %charge_ref.1) | copy-start | bytes 24004
  0.0 19.3 %copy-start.4 = (f32[2000,3]{0,1:T(4,128)S(1)}, f32[2000,3]{0,1:T(4,128)}, u32[]{:S(2)}) copy-start(f32[2000,3]{0,1:T(4,128)} %param.20) | copy-start | bytes 72004
  2.5 19.9 %copy-start.1 = (s32[4096]{0:T(1024)S(1)}, s32[4096]{0:T(1024)}, u32[]{:S(2)}) copy-start(s32[4096]{0:T(1024)} %param.17) | copy-start | bytes 49156
  2.5 36.0 %all-to-all-start = ((f32[128,8,128]{2,1,0:T(8,128)}), f32[128,8,128]{2,1,0:T(8,128)S(1)}, u32[]{:S(2)}, u32[]{:S(2)}) async-start(f32[128,8,128]{2,1,0:T(8,128)} %bitcast.3), calls=%async_computation | async-start | bytes 1048576 | tf_op jit(solution)/shard_map/all_to_all | solution.py:565
  93.5 23.0 %copy-start = (f32[1,2,128,256]{3,2,1,0:T(8,128)S(1)}, f32[1,2,128,256]{3,2,1,0:T(8,128)}, u32[]{:S(2)}) copy-start(f32[1,2,128,256]{3,2,1,0:T(8,128)} %tangent_ref.3) | copy-start | bytes 786436
  93.5 23.0 %copy-start.2 = (bf16[2,144,256]{2,1,0:T(8,128)(2,1)S(1)}, bf16[2,144,256]{2,1,0:T(8,128)(2,1)}, u32[]{:S(2)}) copy-start(bf16[2,144,256]{2,1,0:T(8,128)(2,1)} %constant.34.clone.table_ref) | copy-start | bytes 442372

commit v5 on v4

--- a/solution.py
+++ b/solution.py
@@ -16,11 +16,11 @@
 DISP = 8
 CUT = N // 4
 LINE = 72
-SLABS = 68
-CELLS = SLABS * LINE
+SLABS = 36
+CELLS = SLABS * N
 PAIRS = 40
 TURNED_ROW = PAIRS + CUT
-DUMP = 65 * LINE
+DUMP = 33 * N
 CELL = 40.0
 SLATER = (3.0 / math.pi) ** (1.0 / 3.0)
 FACTOR = (2.0 * math.pi / CELL) ** 2
@@ -30,7 +30,7 @@
 GA_AXES = ("xh", "z")
 PLANE_AXES = ("xl", "yl", "core", "xh", "z")
 SUBS = 8
-PITCH = 136
+PITCH = 264
 GROUPS = 16
 
 f32 = jnp.float32
@@ -78,18 +78,24 @@
     return slot - CUT, (slot <= 2 * CUT).astype(np.float64)
 
 
-def y_inverse_table():
-    frequency, kept = box_frequencies(LINE)
-    angle = angles(frequency, np.arange(N))
-    return (np.concatenate([np.cos(angle), np.sin(angle)], 1) * kept[:, None])
+def y_inverse_table(parity):
+    lane = np.arange(64)
+    angle = angles(np.where(lane <= CUT, lane, lane - 64), np.arange(N))
+    table = np.zeros((N, 2 * N))
+    table[parity * 64 : parity * 64 + 64] = np.concatenate([np.cos(angle), np.sin(angle)], 1)
+    return table
 
 
 def x_inverse_table():
-    across = (4 * np.arange(24)[None, :] + np.arange(4)[:, None]).reshape(-1)
+    parity, slot, step = np.meshgrid(np.arange(2), np.arange(4), np.arange(16), indexing="ij")
+    across = (2 * (4 * step + slot) + parity).reshape(-1)
+    special = across == 65
     kept = (across <= 2 * CUT).astype(np.float64)
     angle = angles(np.arange(N), across - CUT)
     cosine, sine = WEIGHT * np.cos(angle) * kept, WEIGHT * np.sin(angle) * kept
-    return (np.block([[cosine, -sine], [sine, cosine]]))
+    last = np.where(special, -WEIGHT, cosine)
+    cosine = np.where(special, WEIGHT, cosine)
+    return np.block([[cosine, -sine], [sine, last]])
 
 
 def x_forward_table():
@@ -114,7 +120,7 @@
     for group in range(4):
         for part in range(2):
             for entry in range(16):
-                table[group * 32 + entry * 2 + part, group, :, part, entry] = 1.0
+                table[group * 32 + entry // 2 * 4 + part * 2 + entry % 2, group, :, part, entry] = 1.0
     table = table.reshape(N, 2, 2 * N).transpose(1, 0, 2)
     return np.concatenate([table, table], 1).reshape(4 * N, 2 * N)
 
@@ -160,7 +166,8 @@
 def early_tables():
     return packed_tables(
         {
-            "y_inverse": y_inverse_table(),
+            "y_even": y_inverse_table(0),
+            "y_odd": y_inverse_table(1),
             "x_inverse": x_inverse_table(),
             "real": real_table(),
             "real_turned": real_table().T,
@@ -226,6 +233,15 @@
     return across, inplane
 
 
+def box_cell(across, inplane):
+    box = across + CUT
+    special = jnp.logical_and(across == 0, inplane == -CUT)
+    place = jnp.where(special, 64 + CUT, (box & 1) * 64 + (inplane & 63))
+    held = jnp.where(special, CUT, box >> 1)
+    held = jnp.where(across * across + inplane * inplane <= CUT * CUT, held, -1)
+    return place, held, jnp.where(special, -1.0, 1.0)
+
+
 def kept_rows(shape):
     row = lax.broadcasted_iota(jnp.int32, shape, 0)
     return jnp.where(row >= 40, row + 56 - N, row)
@@ -243,7 +259,9 @@
 
 
 def lines_kernel(orbital_ref, tangent_ref, columns_ref, table_ref, out_ref):
-    inside = sphere_radius(own_columns(columns_ref)) <= CUT * CUT
+    own = own_columns(columns_ref)
+    inside = sphere_radius(own) <= CUT * CUT
+    sign = box_cell(*stick_frequencies(own))[2]
     for which, ref in enumerate((orbital_ref, tangent_ref)):
         parts = []
         for part in range(2):
@@ -251,22 +269,19 @@
             parts.append(jnp.where(inside, kept, 0.0))
         lines = dot3(pair(table_ref), halves(jnp.concatenate(parts, 0)))
         for part in range(2):
+            rows = lines[part * N : (part + 1) * N]
+            rows = rows if part == 0 else rows * sign
             for half in range(2):
-                row = half * 4 + which * 2 + part
-                out_ref[pl.ds(row, N, stride=8), :] = lines[part * N : (part + 1) * N, half * N : (half + 1) * N]
-
-
-def circle_reach(slot):
-    across = slot - CUT
-    return math.isqrt(CUT * CUT - across * across) if abs(across) <= CUT else -1
+                out_ref[pl.ds(half * 4 + part * 2 + which, N, stride=8), :] = rows[:, half * N : (half + 1) * N]
 
 
 def fields_kernel(
-    dest_ref, lines_ref, tables, fields_ref, sums_ref, turned, grid, middle
+    dest_ref, lines_ref, tables, sources_ref, fields_ref, sums_ref, turned, grid, found_ref, middle
 ):
     replicate = tables[EARLY_PLACES["replicate"] : EARLY_PLACES["replicate"] + 4 * N, :]
-    lower = lax.broadcasted_iota(jnp.int32, (8, N), 0) < 4
-    for quad in range(4):
+    row = lax.broadcasted_iota(jnp.int32, (8, N), 0)
+    lower = row < 4
+    for quad in range(2):
         for half in range(2):
             tiles = []
             for group in range(4 * quad, 4 * quad + 4):
@@ -282,39 +297,55 @@
                 copies = dot(both, replicate[couple * 2 * N : (couple + 1) * 2 * N])
                 for side in range(2):
                     turned[2 * couple + side, base : base + N, :] = copies[:, side * N : (side + 1) * N]
-    for quad in range(4):
-
-        def scatter(step, carry, quad=quad):
-            for inner in range(8):
-                stick = step * 8 + inner
-                for slot in range(4):
-                    places = dest_ref[(4 * quad + slot) * N + stick]
-                    grid[pl.ds(places & 0xFFFF, 1), :] = turned[slot, pl.ds(quad * 2 * N + stick, 1), :]
-                    grid[pl.ds(places >> 16, 1), :] = turned[slot, pl.ds((quad * 2 + 1) * N + stick, 1), :]
-            return carry
-
-        lax.fori_loop(0, N // 8, scatter, 0)
-    lane = lax.broadcasted_iota(jnp.int32, (LINE, N), 1)
-    distance = jnp.abs(lax.broadcasted_iota(jnp.int32, (LINE, N), 0) - CUT)
+    grid[...] = jnp.zeros_like(grid)
+    found_ref[33 * 32 :, :] = jnp.zeros((3 * 32, N), f32)
+
+    def scatter(word):
+        quad, stick, slot = word // (4 * N), word // 4 % N, word % 4
+        places = dest_ref[(4 * quad + slot) * N + stick]
+        grid[pl.ds(places & 0xFFFF, 1), :] = turned[slot, pl.ds(quad * 2 * N + stick, 1), :]
+        grid[pl.ds(places >> 16, 1), :] = turned[slot, pl.ds((quad * 2 + 1) * N + stick, 1), :]
+
+    upper = jnp.where(lower, 0, -1)
+    word = 0
+    for couple in range(CUT + 1):
+        vectors = jnp.broadcast_to(sources_ref[0, couple : couple + 1, :], (8, N)) + upper
+        index = jnp.broadcast_to(sources_ref[1, couple : couple + 1, :], (8, N))
+        picked = [jnp.zeros((8, N), f32)] * SUBS
+        for group in range(8):
+            mask = vectors == 2 * group + 1
+            for sub in range(SUBS):
+                cells = jnp.take_along_axis(lines_ref[sub * GROUPS + 8 + group], index, axis=1)
+                picked[sub] = jnp.where(mask, cells, picked[sub])
+                if sub % 2 == 1 and word < 8 * N:
+                    scatter(word)
+                    word += 1
+        picked = [part + pltpu.roll(part, 4, 0) for part in picked]
+        for four in range(2):
+            a, b, c, d = picked[4 * four : 4 * four + 4]
+            real = jnp.where(row < 2, a, jnp.where(lower, pltpu.roll(b, 2, 0), jnp.where(row < 6, c, pltpu.roll(d, 2, 0))))
+            imag = jnp.where(row < 2, pltpu.roll(a, 6, 0), jnp.where(lower, b, jnp.where(row < 6, pltpu.roll(c, 6, 0), d)))
+            base = couple * 32 + four * 8
+            found_ref[base : base + 8, :] = real
+            found_ref[base + 16 : base + 24, :] = imag
+    lane = lax.broadcasted_iota(jnp.int32, (N, N), 1)
     masks = [lane // 32 == slot for slot in range(4)]
-    for step in range(17, 24):
-        middle[step * PITCH : step * PITCH + N, :] = jnp.zeros((N, N), f32)
-    ytable = early_table(tables, "y_inverse")
-    for step in range(17):
+    for step in range(9, 16):
+        middle[step * PITCH : step * PITCH + 2 * N, :] = jnp.zeros((2 * N, N), f32)
+    ytables = [early_table(tables, "y_even"), early_table(tables, "y_odd")]
+    for step in range(9):
         packed = None
         for slot in range(4):
-            slab = grid[(4 * step + slot) * LINE : (4 * step + slot + 1) * LINE, :]
+            slab = grid[(4 * step + slot) * N : (4 * step + slot + 1) * N, :]
             packed = slab if packed is None else jnp.where(masks[slot], slab, packed)
-        reach = jnp.full((1, N), circle_reach(4 * step), jnp.int32)
-        for slot in range(1, 4):
-            reach = jnp.where(masks[slot][0:1], circle_reach(4 * step + slot), reach)
-        packed = jnp.where(distance <= reach, packed, 0.0)
-        lines = dot3(halves(packed.T), ytable)
-        for slot in range(4):
-            real, imag = lines[slot * 32 : slot * 32 + 16], lines[slot * 32 + 16 : slot * 32 + 32]
-            base = step * PITCH + slot * 16
-            middle[base : base + 16, :] = real[:, 0:N] - imag[:, N : 2 * N]
-            middle[base + 64 : base + 80, :] = real[:, N : 2 * N] + imag[:, 0:N]
+        lines = halves(packed.T + found_ref[step * N : (step + 1) * N, :])
+        for parity in range(2):
+            done = dot3(lines, ytables[parity])
+            for slot in range(4):
+                real, imag = done[slot * 32 : slot * 32 + 16], done[slot * 32 + 16 : slot * 32 + 32]
+                base = step * PITCH + parity * N + slot * 16
+                middle[base : base + 16, :] = real[:, 0:N] - imag[:, N : 2 * N]
+                middle[base + 64 : base + 80, :] = real[:, N : 2 * N] + imag[:, 0:N]
     density = jnp.zeros((N, N), f32)
     response = jnp.zeros((N, N), f32)
     xtable = early_table(tables, "x_inverse")
@@ -323,8 +354,10 @@
         for which in range(2):
             rows = []
             for part in range(2):
-                for slot in range(4):
-                    rows.append(middle[pl.ds(part * 64 + slot * 16 + band * 2 + which, 24, stride=PITCH), :])
+                for parity in range(2):
+                    for slot in range(4):
+                        base = parity * N + part * 64 + slot * 16 + band * 2 + which
+                        rows.append(middle[pl.ds(base, 16, stride=PITCH), :])
             sides.append(jnp.concatenate(rows, 0))
         field = dot3(xtable, halves(jnp.concatenate(sides, 1)))
         fields_ref[band] = field
@@ -405,9 +438,11 @@
     early_ref,
     late_ref,
     lines_ref,
+    columns_ref,
     out_ref,
     early_out,
     late_out,
+    sources_ref,
     centres,
     spreads,
     marks,
@@ -449,6 +484,18 @@
     left = jnp.concatenate([along_x, padding], 0).T
     right = jnp.concatenate([scaled, padding], 0)
     out_ref[2] = dot3(halves(left), halves(right))
+    place, held, ignored = box_cell(*stick_frequencies(columns_ref[GROUPS : 2 * GROUPS, :]))
+    pairs = lax.broadcasted_iota(jnp.int32, (PAIRS, N), 0)
+    lanes = lax.broadcasted_iota(jnp.int32, (PAIRS, N), 1).astype(f32)
+    places = lax.broadcasted_iota(jnp.int32, (N, N), 0)
+    found = jnp.zeros((2 * PAIRS, N), f32)
+    for vector in range(GROUPS):
+        here = held[vector : vector + 1] == pairs
+        marks = jnp.concatenate([jnp.where(here, vector + 1.0, 0.0), jnp.where(here, lanes, 0.0)], 0).astype(bf16)
+        spots = jnp.where(place[vector : vector + 1] == places, 1.0, 0.0).astype(bf16)
+        found = found + dot(marks, spots, ((1,), (1,)))
+    sources_ref[0] = found[0:PAIRS].astype(jnp.int32)
+    sources_ref[1] = found[PAIRS : 2 * PAIRS].astype(jnp.int32)
     for copy in copies:
         copy.wait()
 
@@ -489,12 +536,7 @@
             at = (couple * 2 + part) * SUBS
             cells[at : at + SUBS, :] = lines[pl.ds(part * SUBS * PAIRS + couple, SUBS, stride=PAIRS), :]
     across, inplane = stick_frequencies(columns_ref[...])
-    box = across + CUT
-    special = jnp.logical_and(across == 0, inplane == -CUT)
-    place = jnp.where(special, 64 + CUT, (box & 1) * 64 + (inplane & 63))
-    held = jnp.where(special, CUT, box >> 1)
-    held = jnp.where(across * across + inplane * inplane <= CUT * CUT, held, -1)
-    sign = jnp.where(special, -1.0, 1.0)
+    place, held, sign = box_cell(across, inplane)
     for vector in range(2 * GROUPS):
         index = jnp.broadcast_to(place[vector : vector + 1], (SUBS, N))
         wanted = jnp.broadcast_to(held[vector : vector + 1], (SUBS, N))
@@ -579,17 +621,17 @@
 ):
     columns = stick_columns.reshape(STICKS // N, N)
     across, inplane = stick_frequencies(stick_columns)
-    cell = (across + CUT) * LINE + (inplane + CUT)
-    dest = jnp.where(across * across + inplane * inplane <= CUT * CUT, cell, DUMP).reshape(GROUPS, 2, N)
+    place, held, ignored = box_cell(across, inplane)
+    dest = jnp.where(held >= 0, held * N + place, DUMP).reshape(GROUPS, 2, N)[:8]
     dest = (dest[:, 0] + dest[:, 1] * 65536).reshape(-1)
     lines = call(lines_kernel, pltpu.VMEM((N * 8, N), f32), vmem(4), 8)(
         stay(orbitals), stay(orbital_tangent), stay(columns), stay(z_inverse_table())
     )
     arrived = exchange(lines.reshape(N, 8, N), PLANE_AXES)
-    planes, early, late = call(
+    planes, early, late, sources = call(
         ions_kernel,
-        (pltpu.VMEM((3, N, N), f32), pltpu.VMEM(EARLY.shape, bf16), pltpu.VMEM(LATE.shape, bf16)),
-        smem(5) + vmem(1) + anywhere(5),
+        (pltpu.VMEM((3, N, N), f32), pltpu.VMEM(EARLY.shape, bf16), pltpu.VMEM(LATE.shape, bf16), pltpu.VMEM((2, PAIRS, N), jnp.int32)),
+        smem(5) + vmem(1) + anywhere(5) + vmem(1),
         8,
         [pltpu.VMEM((24, N), f32)] * 3 + [pltpu.VMEM((8, N), f32), pltpu.SemaphoreType.DMA((4,))],
     )(
@@ -604,18 +646,20 @@
         stay(EARLY),
         stay(LATE),
         lines,
+        columns,
     )
     fields, sums = call(
         fields_kernel,
         (shape(SUBS, 2 * N, 2 * N), shape(2 * N, N)),
-        smem(1) + vmem(2),
+        smem(1) + vmem(3),
         20,
         [
-            pltpu.VMEM((4, 8 * N, N), f32),
+            pltpu.VMEM((4, 4 * N, N), f32),
             pltpu.VMEM((CELLS, N), f32),
-            pltpu.VMEM((24 * PITCH, N), f32),
+            pltpu.VMEM((SLABS * 32, N), f32),
+            pltpu.VMEM((16 * PITCH, N), f32),
         ],
-    )(dest, arrived, early)
+    )(dest, arrived, early, sources)
     sums = exchange(sums.reshape(64, 4, N), BAND_AXES + ("xh",)).reshape(2 * N, N)
     sums, spectrum = call(mix_kernel, (shape(64, N), shape(2 * N, N)), vmem(1), 4)(sums)
     spectrum = exchange(spectrum.reshape(8, 32, N), "z").reshape(2 * N, N)

time: 118 us -> 116 us (0.983)
  Pallas kernels: 18.6 us -> 17.4 us
    pallas_call x1, Pallas kernels: 7.28 us -> 6.01 us  [body(): call(fields_kernel, (shape(SUBS, 2 * N, 2 * N), shape(2 * N, N)), smem(1)...]
where the time goes in v5:
time: 116 us
  blocking collectives  65.7 us (57%)
  Pallas kernels  17.4 us (15%)
  starting transfers between devices  16.6 us (14%)
  waiting for transfers between devices  16 us (14%)
    all_to_all x4, blocking collectives, exchange(): return lax.all_to_all(values, axes, 0, 0, tiled=True)  65.7 us
    all_to_all x1, starting transfers between devices, exchange(): return lax.all_to_all(values, axes, 0, 0, tiled=True)  16.6 us
    all_to_all x1, waiting for transfers between devices, exchange(): return lax.all_to_all(values, axes, 0, 0, tiled=True)  16 us
    pallas_call x1, Pallas kernels, body(): call(fields_kernel, (shape(SUBS, 2 * N, 2 * N), shape(2 * N, N)), smem(1)...  6.01 us
    pallas_call x1, Pallas kernels, body(): call(products_kernel, shape(4 * N, N), vmem(5), 20, [pltpu.VMEM((16 * PAI...  4.42 us
    pallas_call x1, Pallas kernels, body(): call(ions_kernel, (pltpu.VMEM((3, N, N), f32), pltpu.VMEM(EARLY.shape, bf...  3.13 us
    pallas_call x1, Pallas kernels, body(): call(lines_kernel, pltpu.VMEM((N * 8, N), f32), vmem(4), 8)  2.42 us
  transfers between devices with their start and end apart: 1, of which 1 were waited for; matrix products, arithmetic and copies ran while one was open for 0% of the time, Pallas kernels for 3%

profile of v5, /device:TPU:1, one launch (start us, length us, event | category | flops | bytes accessed | tf_op | source)
XLA Modules:
  0.0 115.9 jit_solution(5433604271569783486)
XLA Ops:
  0.0 0.0 copy-start.3
  0.0 0.0 copy-start.1
  0.0 0.0 copy-start.8
  0.0 0.0 copy-start.7
  0.0 0.0 copy-start.6
  0.0 0.0 copy-start.5
  0.0 0.0 copy-start.4
  0.0 2.4 %lines.1.lines_ref = f32[1024,128]{1,0:T(8,128)} custom-call(f32[1,2,128,256]{3,2,1,0:T(8,128)} %orbital_ref.1, f32[1,2,128,256]{3,2,1,0:T(8,128)} %tangent_ref.3, s32[32,128]{1,0:T(8,128)} %bitcast.17, bf16[2,256,144]{2,1,0:T(8,128)(2,1)} %constant.42.clone.table_ref), custom_call_target="tpu_custom_call" | custom-call | tf_op jit(solution)/shard_map/lines/pallas_call | solution.py:627
  2.5 16.6 %all-to-all-start = ((f32[128,8,128]{2,1,0:T(8,128)}), f32[128,8,128]{2,1,0:T(8,128)S(1)}, u32[]{:S(2)}, u32[]{:S(2)}) async-start(f32[128,8,128]{2,1,0:T(8,128)} %bitcast.3), calls=%async_computation | async-start | bytes 1048576 | tf_op jit(solution)/shard_map/all_to_all | solution.py:607
  19.1 0.0 copy-done.3
  19.1 0.0 copy-done.1
  19.1 0.0 copy-done.8
  19.1 0.0 copy-done.7
  19.2 0.0 copy-done.6
  19.2 0.0 copy-done.5
  19.2 0.0 copy-done.4
  19.2 3.1 %ions.1 = (f32[3,128,128]{2,1,0:T(8,128)S(1)}, bf16[2048,256]{1,0:T(8,128)(2,1)S(1)}, bf16[1600,256]{1,0:T(8,128)(2,1)S(1)}, s32[2,40,128]{2,1,0:T(8,128)S(1)}) custom-call(s32[8]{0:T(128)S(1)} %copy-done.7, s32[8]{0:T(128)S(1)} %copy-done.8, f32[3,2000]{1,0:T(4,128)S(1)} %bitcast.25, f32[2000]{0:T(1024)S(1)} %copy-done.5, f32[2000]{0:T(1024)S(1)} %copy-done.6, ...), custom_call_target="tpu_custom_call" | custom-call | tf_op jit(solution)/shard_map/ions/pallas_call | solution.py:631
  22.4 16.0 %all-to-all-done.lines_ref = f32[128,8,128]{2,1,0:T(8,128)S(1)} async-done(((f32[128,8,128]{2,1,0:T(8,128)}), f32[128,8,128]{2,1,0:T(8,128)S(1)}, u32[]{:S(2)}, u32[]{:S(2)}) %all-to-all-start) | async-done | bytes 524320 | tf_op jit(solution)/shard_map/all_to_all | solution.py:607
  38.4 6.0 %fields.1 = (f32[8,256,256]{2,1,0:T(8,128)S(1)}, f32[256,128]{1,0:T(8,128)S(1)}) custom-call(s32[1024]{0:T(1024)S(1)} %bitcast.26, f32[128,8,128]{2,1,0:T(8,128)S(1)} %all-to-all-done.lines_ref, bf16[2048,256]{1,0:T(8,128)(2,1)S(1)} %get-tuple-element.13.tables, s32[2,40,128]{2,1,0:T(8,128)S(1)} %get-tuple-element.14.sources_ref), custom_call_target="tpu_custom_call" | custom-call | tf_op jit(solution)/shard_map/fields/pallas_call | solution.py:651
  44.4 19.3 %all_to_all.25 = f32[64,4,128]{2,1,0:T(4,128)S(1)} all-to-all(f32[64,4,128]{2,1,0:T(4,128)S(1)} %bitcast.23), channel_id=1, replica_groups=mesh['xl'=2,'yh'=4,'yl'=2,'core'=2,'xh'=2,'z'=8] {'xl','yh','yl','core',..., dimensions={0} | all-to-all | bytes 262144 | tf_op jit(solution)/shard_map/all_to_all | solution.py:607
  63.7 10.8 %all_to_all.26 = f32[8,32,128]{2,1,0:T(8,128)S(1)} all-to-all(f32[8,32,128]{2,1,0:T(8,128)S(1)} %bitcast.24), channel_id=1, replica_groups=mesh['xl'=2,'yh'=4,'yl'=2,'core'=2,'xh'=2,'z'=8] {'z'}, dimensions={0} | all-to-all | bytes 262144 | tf_op jit(solution)/shard_map/all_to_all | solution.py:607
  74.4 0.4 hartree.1
  74.9 17.2 %all_to_all.27 = f32[64,3,2,128]{3,2,1,0:T(2,128)S(1)} all-to-all(f32[64,3,2,128]{3,2,1,0:T(2,128)S(1)} %bitcast.16), channel_id=1, replica_groups=mesh['xl'=2,'yh'=4,'yl'=2,'core'=2,'xh'=2,'z'=8] {'xl','yh','yl','core',..., dimensions={0} | all-to-all | bytes 393216 | tf_op jit(solution)/shard_map/all_to_all | solution.py:607
  92.1 0.0 copy-start
  92.1 0.0 copy-start.2
  92.1 4.4 %products.1 = f32[512,128]{1,0:T(8,128)S(1)} custom-call(s32[32,128]{1,0:T(8,128)S(1)} %bitcast.19, f32[8,256,256]{2,1,0:T(8,128)S(1)} %get-tuple-element.15.fields_ref, f32[384,128]{1,0:T(8,128)S(1)} %bitcast.15, f32[3,128,128]{2,1,0:T(8,128)S(1)} %get-tuple-element.20.planes_ref, bf16[1600,256]{1,0:T(8,128)(2,1)S(1)} %get-tuple-element.19.tables_ref), custom_call_target="tpu_custom_call" | custom-call | tf_op jit(solution)/shard_map/products/pallas_call | solution.py:668
  96.5 18.5 %all_to_all.28 = f32[128,4,128]{2,1,0:T(4,128)S(1)} all-to-all(f32[128,4,128]{2,1,0:T(4,128)S(1)} %bitcast.13), channel_id=1, replica_groups=mesh['xl'=2,'yh'=4,'yl'=2,'core'=2,'xh'=2,'z'=8] {'xl','yl','core','xh',..., dimensions={0} | all-to-all | bytes 524288 | tf_op jit(solution)/shard_map/all_to_all | solution.py:607
  115.0 0.0 copy-done
  115.0 0.0 copy-done.2
  115.0 0.9 result.1
  (5 shorter events, 0.1 us)
Async XLA Ops:
  0.0 19.1 %copy-start.3 = (bf16[2,256,128]{2,1,0:T(8,128)(2,1)S(1)}, bf16[2,256,128]{2,1,0:T(8,128)(2,1)}, u32[]{:S(2)}) copy-start(bf16[2,256,128]{2,1,0:T(8,128)(2,1)} %constant.45.clone.table_ref) | copy-start | bytes 393220
  0.0 19.1 %copy-start.1 = (s32[4096]{0:T(1024)S(1)}, s32[4096]{0:T(1024)}, u32[]{:S(2)}) copy-start(s32[4096]{0:T(1024)} %param.17) | copy-start | bytes 49156
  0.0 19.1 %copy-start.8 = (s32[8]{0:T(128)S(1)}, s32[8]{0:T(128)}, u32[]{:S(2)}) copy-start(s32[8]{0:T(128)} %direction_ref.1) | copy-start | bytes 100
  0.0 19.1 %copy-start.7 = (s32[8]{0:T(128)S(1)}, s32[8]{0:T(128)}, u32[]{:S(2)}) copy-start(s32[8]{0:T(128)} %atom_ref.1) | copy-start | bytes 100
  0.0 19.1 %copy-start.6 = (f32[2000]{0:T(1024)S(1)}, f32[2000]{0:T(1024)}, u32[]{:S(2)}) copy-start(f32[2000]{0:T(1024)} %widths_ref.1) | copy-start | bytes 24004
  0.0 19.1 %copy-start.5 = (f32[2000]{0:T(1024)S(1)}, f32[2000]{0:T(1024)}, u32[]{:S(2)}) copy-start(f32[2000]{0:T(1024)} %charge_ref.1) | copy-start | bytes 24004
  0.0 19.1 %copy-start.4 = (f32[2000,3]{0,1:T(4,128)S(1)}, f32[2000,3]{0,1:T(4,128)}, u32[]{:S(2)}) copy-start(f32[2000,3]{0,1:T(4,128)} %param.20) | copy-start | bytes 72004
  2.5 35.9 %all-to-all-start = ((f32[128,8,128]{2,1,0:T(8,128)}), f32[128,8,128]{2,1,0:T(8,128)S(1)}, u32[]{:S(2)}, u32[]{:S(2)}) async-start(f32[128,8,128]{2,1,0:T(8,128)} %bitcast.3), calls=%async_computation | async-start | bytes 1048576 | tf_op jit(solution)/shard_map/all_to_all | solution.py:607
  92.1 22.9 %copy-start = (f32[1,2,128,256]{3,2,1,0:T(8,128)S(1)}, f32[1,2,128,256]{3,2,1,0:T(8,128)}, u32[]{:S(2)}) copy-start(f32[1,2,128,256]{3,2,1,0:T(8,128)} %tangent_ref.3) | copy-start | bytes 786436
  92.1 22.9 %copy-start.2 = (bf16[2,144,256]{2,1,0:T(8,128)(2,1)S(1)}, bf16[2,144,256]{2,1,0:T(8,128)(2,1)}, u32[]{:S(2)}) copy-start(bf16[2,144,256]{2,1,0:T(8,128)(2,1)} %constant.46.clone.table_ref) | copy-start | bytes 442372

commit v6 on v5

--- a/solution.py
+++ b/solution.py
@@ -514,6 +514,7 @@
     change = exchange / (3.0 * total) * response + hartree + planes_ref[2]
     xtable = late_table(tables_ref, "x_forward")
     ytable = late_table(tables_ref, "y_forward")
+    ytwice = jnp.concatenate([ytable[0], ytable[0]], 0)
     effective2 = jnp.concatenate([effective, effective], 0)
     change2 = jnp.concatenate([change, change], 0)
     lower = lax.broadcasted_iota(jnp.int32, (PAIRS, N), 1) < 64
@@ -523,7 +524,8 @@
             sides.append(effective2 * fields_ref[band, :, N : 2 * N] + change2 * fields_ref[band, :, 0:N])
         across = dot3(xtable, halves(jnp.concatenate(sides, 1)))
         rows = jnp.concatenate([across[:, 0:N], across[:, N : 2 * N]], 0)
-        done = dot3(halves(rows), ytable)
+        high, low = halves(rows)
+        done = dot(jnp.concatenate([high, low], 1), ytwice) + dot(high, ytable[1])
         for side in range(2):
             real = done[side * 4 * PAIRS : side * 4 * PAIRS + 2 * PAIRS]
             imag = done[side * 4 * PAIRS + 2 * PAIRS : (side + 1) * 4 * PAIRS]

time: 116 us -> 116 us (level)
  no operation moved by 1% of the time
where the time goes in v6:
time: 116 us
  blocking collectives  65.7 us (57%)
  Pallas kernels  17.2 us (15%)
  starting transfers between devices  16.6 us (14%)
  waiting for transfers between devices  16 us (14%)
    all_to_all x4, blocking collectives, exchange(): return lax.all_to_all(values, axes, 0, 0, tiled=True)  65.7 us
    all_to_all x1, starting transfers between devices, exchange(): return lax.all_to_all(values, axes, 0, 0, tiled=True)  16.6 us
    all_to_all x1, waiting for transfers between devices, exchange(): return lax.all_to_all(values, axes, 0, 0, tiled=True)  16 us
    pallas_call x1, Pallas kernels, body(): call(fields_kernel, (shape(SUBS, 2 * N, 2 * N), shape(2 * N, N)), smem(1)...  6.01 us
    pallas_call x1, Pallas kernels, body(): call(products_kernel, shape(4 * N, N), vmem(5), 20, [pltpu.VMEM((16 * PAI...  4.24 us
    pallas_call x1, Pallas kernels, body(): call(ions_kernel, (pltpu.VMEM((3, N, N), f32), pltpu.VMEM(EARLY.shape, bf...  3.13 us
    pallas_call x1, Pallas kernels, body(): call(lines_kernel, pltpu.VMEM((N * 8, N), f32), vmem(4), 8)  2.42 us
  transfers between devices with their start and end apart: 1, of which 1 were waited for; matrix products, arithmetic and copies ran while one was open for 0% of the time, Pallas kernels for 3%

profile of v6, /device:TPU:1, one launch (start us, length us, event | category | flops | bytes accessed | tf_op | source)
XLA Modules:
  0.0 115.8 jit_solution(16519164539877604443)
XLA Ops:
  0.0 0.0 copy-start.3
  0.0 0.0 copy-start.1
  0.0 0.0 copy-start.8
  0.0 0.0 copy-start.7
  0.0 0.0 copy-start.6
  0.0 0.0 copy-start.5
  0.0 0.0 copy-start.4
  0.0 2.4 %lines.1.lines_ref = f32[1024,128]{1,0:T(8,128)} custom-call(f32[1,2,128,256]{3,2,1,0:T(8,128)} %orbital_ref.1, f32[1,2,128,256]{3,2,1,0:T(8,128)} %tangent_ref.3, s32[32,128]{1,0:T(8,128)} %bitcast.17, bf16[2,256,144]{2,1,0:T(8,128)(2,1)} %constant.42.clone.table_ref), custom_call_target="tpu_custom_call" | custom-call | tf_op jit(solution)/shard_map/lines/pallas_call | solution.py:629
  2.5 16.6 %all-to-all-start = ((f32[128,8,128]{2,1,0:T(8,128)}), f32[128,8,128]{2,1,0:T(8,128)S(1)}, u32[]{:S(2)}, u32[]{:S(2)}) async-start(f32[128,8,128]{2,1,0:T(8,128)} %bitcast.3), calls=%async_computation | async-start | bytes 1048576 | tf_op jit(solution)/shard_map/all_to_all | solution.py:609
  19.1 0.0 copy-done.3
  19.1 0.0 copy-done.1
  19.1 0.0 copy-done.8
  19.1 0.0 copy-done.7
  19.2 0.0 copy-done.6
  19.2 0.0 copy-done.5
  19.2 0.0 copy-done.4
  19.2 3.1 %ions.1 = (f32[3,128,128]{2,1,0:T(8,128)S(1)}, bf16[2048,256]{1,0:T(8,128)(2,1)S(1)}, bf16[1600,256]{1,0:T(8,128)(2,1)S(1)}, s32[2,40,128]{2,1,0:T(8,128)S(1)}) custom-call(s32[8]{0:T(128)S(1)} %copy-done.7, s32[8]{0:T(128)S(1)} %copy-done.8, f32[3,2000]{1,0:T(4,128)S(1)} %bitcast.25, f32[2000]{0:T(1024)S(1)} %copy-done.5, f32[2000]{0:T(1024)S(1)} %copy-done.6, ...), custom_call_target="tpu_custom_call" | custom-call | tf_op jit(solution)/shard_map/ions/pallas_call | solution.py:633
  22.4 16.0 %all-to-all-done.lines_ref = f32[128,8,128]{2,1,0:T(8,128)S(1)} async-done(((f32[128,8,128]{2,1,0:T(8,128)}), f32[128,8,128]{2,1,0:T(8,128)S(1)}, u32[]{:S(2)}, u32[]{:S(2)}) %all-to-all-start) | async-done | bytes 524320 | tf_op jit(solution)/shard_map/all_to_all | solution.py:609
  38.4 6.0 %fields.1 = (f32[8,256,256]{2,1,0:T(8,128)S(1)}, f32[256,128]{1,0:T(8,128)S(1)}) custom-call(s32[1024]{0:T(1024)S(1)} %bitcast.26, f32[128,8,128]{2,1,0:T(8,128)S(1)} %all-to-all-done.lines_ref, bf16[2048,256]{1,0:T(8,128)(2,1)S(1)} %get-tuple-element.13.tables, s32[2,40,128]{2,1,0:T(8,128)S(1)} %get-tuple-element.14.sources_ref), custom_call_target="tpu_custom_call" | custom-call | tf_op jit(solution)/shard_map/fields/pallas_call | solution.py:653
  44.4 19.3 %all_to_all.25 = f32[64,4,128]{2,1,0:T(4,128)S(1)} all-to-all(f32[64,4,128]{2,1,0:T(4,128)S(1)} %bitcast.23), channel_id=1, replica_groups=mesh['xl'=2,'yh'=4,'yl'=2,'core'=2,'xh'=2,'z'=8] {'xl','yh','yl','core',..., dimensions={0} | all-to-all | bytes 262144 | tf_op jit(solution)/shard_map/all_to_all | solution.py:609
  63.7 10.8 %all_to_all.26 = f32[8,32,128]{2,1,0:T(8,128)S(1)} all-to-all(f32[8,32,128]{2,1,0:T(8,128)S(1)} %bitcast.24), channel_id=1, replica_groups=mesh['xl'=2,'yh'=4,'yl'=2,'core'=2,'xh'=2,'z'=8] {'z'}, dimensions={0} | all-to-all | bytes 262144 | tf_op jit(solution)/shard_map/all_to_all | solution.py:609
  74.4 0.4 hartree.1
  74.9 17.2 %all_to_all.27 = f32[64,3,2,128]{3,2,1,0:T(2,128)S(1)} all-to-all(f32[64,3,2,128]{3,2,1,0:T(2,128)S(1)} %bitcast.16), channel_id=1, replica_groups=mesh['xl'=2,'yh'=4,'yl'=2,'core'=2,'xh'=2,'z'=8] {'xl','yh','yl','core',..., dimensions={0} | all-to-all | bytes 393216 | tf_op jit(solution)/shard_map/all_to_all | solution.py:609
  92.1 0.0 copy-start
  92.1 0.0 copy-start.2
  92.1 4.2 %products.1 = f32[512,128]{1,0:T(8,128)S(1)} custom-call(s32[32,128]{1,0:T(8,128)S(1)} %bitcast.19, f32[8,256,256]{2,1,0:T(8,128)S(1)} %get-tuple-element.15.fields_ref, f32[384,128]{1,0:T(8,128)S(1)} %bitcast.15, f32[3,128,128]{2,1,0:T(8,128)S(1)} %get-tuple-element.20.planes_ref, bf16[1600,256]{1,0:T(8,128)(2,1)S(1)} %get-tuple-element.19.tables_ref), custom_call_target="tpu_custom_call" | custom-call | tf_op jit(solution)/shard_map/products/pallas_call | solution.py:670
  96.3 18.5 %all_to_all.28 = f32[128,4,128]{2,1,0:T(4,128)S(1)} all-to-all(f32[128,4,128]{2,1,0:T(4,128)S(1)} %bitcast.13), channel_id=1, replica_groups=mesh['xl'=2,'yh'=4,'yl'=2,'core'=2,'xh'=2,'z'=8] {'xl','yl','core','xh',..., dimensions={0} | all-to-all | bytes 524288 | tf_op jit(solution)/shard_map/all_to_all | solution.py:609
  114.8 0.0 copy-done
  114.8 0.0 copy-done.2
  114.8 0.9 result.1
  (5 shorter events, 0.1 us)
Async XLA Ops:
  0.0 19.1 %copy-start.3 = (bf16[2,256,128]{2,1,0:T(8,128)(2,1)S(1)}, bf16[2,256,128]{2,1,0:T(8,128)(2,1)}, u32[]{:S(2)}) copy-start(bf16[2,256,128]{2,1,0:T(8,128)(2,1)} %constant.45.clone.table_ref) | copy-start | bytes 393220
  0.0 19.1 %copy-start.1 = (s32[4096]{0:T(1024)S(1)}, s32[4096]{0:T(1024)}, u32[]{:S(2)}) copy-start(s32[4096]{0:T(1024)} %param.17) | copy-start | bytes 49156
  0.0 19.1 %copy-start.8 = (s32[8]{0:T(128)S(1)}, s32[8]{0:T(128)}, u32[]{:S(2)}) copy-start(s32[8]{0:T(128)} %direction_ref.1) | copy-start | bytes 100
  0.0 19.1 %copy-start.7 = (s32[8]{0:T(128)S(1)}, s32[8]{0:T(128)}, u32[]{:S(2)}) copy-start(s32[8]{0:T(128)} %atom_ref.1) | copy-start | bytes 100
  0.0 19.1 %copy-start.6 = (f32[2000]{0:T(1024)S(1)}, f32[2000]{0:T(1024)}, u32[]{:S(2)}) copy-start(f32[2000]{0:T(1024)} %widths_ref.1) | copy-start | bytes 24004
  0.0 19.1 %copy-start.5 = (f32[2000]{0:T(1024)S(1)}, f32[2000]{0:T(1024)}, u32[]{:S(2)}) copy-start(f32[2000]{0:T(1024)} %charge_ref.1) | copy-start | bytes 24004
  0.0 19.1 %copy-start.4 = (f32[2000,3]{0,1:T(4,128)S(1)}, f32[2000,3]{0,1:T(4,128)}, u32[]{:S(2)}) copy-start(f32[2000,3]{0,1:T(4,128)} %param.20) | copy-start | bytes 72004
  2.5 35.9 %all-to-all-start = ((f32[128,8,128]{2,1,0:T(8,128)}), f32[128,8,128]{2,1,0:T(8,128)S(1)}, u32[]{:S(2)}, u32[]{:S(2)}) async-start(f32[128,8,128]{2,1,0:T(8,128)} %bitcast.3), calls=%async_computation | async-start | bytes 1048576 | tf_op jit(solution)/shard_map/all_to_all | solution.py:609
  92.1 22.8 %copy-start = (f32[1,2,128,256]{3,2,1,0:T(8,128)S(1)}, f32[1,2,128,256]{3,2,1,0:T(8,128)}, u32[]{:S(2)}) copy-start(f32[1,2,128,256]{3,2,1,0:T(8,128)} %tangent_ref.3) | copy-start | bytes 786436
  92.1 22.8 %copy-start.2 = (bf16[2,144,256]{2,1,0:T(8,128)(2,1)S(1)}, bf16[2,144,256]{2,1,0:T(8,128)(2,1)}, u32[]{:S(2)}) copy-start(bf16[2,144,256]{2,1,0:T(8,128)(2,1)} %constant.46.clone.table_ref) | copy-start | bytes 442372
